TPU v7x, 256 devices: a whole 4x4x8 slice. The times are simulated.
256 devices in a mesh: seq: 64 (over x, y, z_hi), row: 2 (over z_lo), col: 2 (over core).
Axes of the slice: x: 4, y: 4, z: 8 (z_hi: 4, z_lo: 2; z = z_hi * 2 + z_lo), core: 2. Of those that a mesh axis runs over, the one named last changes fastest.
Arguments:
- layer_input: bfloat16 [8192, 4096], P('seq', ('row', 'col')), may hold values from -6 to 6
- attn_out: bfloat16 [8192, 8192], P(('row', 'col'), 'seq'), may hold values from -6 to 6
- out_grad: bfloat16 [8192, 4096], P('seq', ('row', 'col')), may hold values from -0.3125 to 0.3125
- q_grad: bfloat16 [8192, 8192], P(('row', 'col'), 'seq'), may hold values from -0.875 to 0.875
- k_grad: bfloat16 [8192, 8192], P(('row', 'col'), 'seq'), may hold values from -0.3125 to 0.3125
- q_weight: bfloat16 [4096, 8192], P(('row', 'col'), 'seq'), may hold values from -0.375 to 0.375
- k_weight: bfloat16 [64, 512, 128], P('seq', ('row', 'col')), may hold values from -0.375 to 0.375
- o_weight: bfloat16 [8192, 4096], P('seq', ('row', 'col')), may hold values from -0.375 to 0.375
Outputs:
- input_grad: bfloat16 [8192, 4096], P('seq', ('row', 'col'))
- attn_grad: bfloat16 [8192, 8192], P(('row', 'col'), 'seq')
- q_weight_grad: float32 [4096, 8192], P(('row', 'col'), 'seq')
- k_weight_grad: float32 [64, 512, 128], P('seq', ('row', 'col'))
- o_weight_grad: float32 [8192, 4096], P('seq', ('row', 'col'))
All inputs are finite; a program needn't handle non-finite values.
Results may differ from a plain program's by a relative error of at most 0.001.
Values may be sent and summed in bfloat16 or wider, within the bound.
A program may use at most 192 MiB of HBM per device.

v0:
```python
import jax
import jax.numpy as jnp
from jax import lax
from jax.sharding import PartitionSpec as P

QUERIES_PER_KEY = 8


def swapped(value, axis, stride):
    return lax.ppermute(value, axis, [(i, i ^ 1 << stride) for i in range(lax.axis_size(axis))])


def shards(layer_input, attn_out, out_grad, q_grad, k_grad, q_weight, k_weight, o_weight):
    head_out, head_q, head_k = (
        lax.all_gather(attn_out, ("row", "col"), axis=0, tiled=True),
        lax.all_gather(q_grad, ("row", "col"), axis=0, tiled=True),
        lax.all_gather(k_grad, ("row", "col"), axis=0, tiled=True),
    )
    grads_cat = jnp.concatenate([head_q, head_k], axis=1)
    head_size = q_weight.shape[1]
    group_bits = QUERIES_PER_KEY.bit_length() - 1
    position = lax.axis_index("seq")
    stacked = k_weight[0]
    for level in range(group_bits):
        partner = swapped(stacked, "seq", level)
        upper = position >> level & 1 == 1
        stacked = jnp.where(
            upper,
            jnp.concatenate([partner, stacked], axis=0),
            jnp.concatenate([stacked, partner], axis=0),
        )
    weight_cat = jnp.concatenate([q_weight, stacked], axis=1)
    portion = lax.all_gather(out_grad, "seq", axis=0, tiled=True)
    used = head_out
    o_total = lax.dot_general(
        used, portion, (((0,), (0,)), ((), ())), preferred_element_type=jnp.float32
    )
    product = lax.dot_general(
        portion, o_weight, (((1,), (1,)), ((), ())), preferred_element_type=jnp.float32
    )
    attn_part = product
    out_totals = (o_total, attn_part)
    used = grads_cat
    weight_sums = lax.dot_general(
        lax.all_gather(layer_input, "seq", axis=0, tiled=True),
        used,
        (((0,), (0,)), ((), ())),
        preferred_element_type=jnp.float32,
    )
    weight_sums, out_totals = (weight_sums, out_totals)
    used = grads_cat
    input_grad = lax.psum_scatter(
        lax.dot_general(
            used, weight_cat, (((1,), (1,)), ((), ())), preferred_element_type=jnp.float32
        ),
        "seq",
        scatter_dimension=0,
        tiled=True,
    ).astype(jnp.bfloat16)
    o_weight_grad, attn_part = out_totals
    attn_grad = lax.psum_scatter(attn_part, ("row", "col"), scatter_dimension=0, tiled=True).astype(
        jnp.bfloat16
    )
    q_weight_grad = weight_sums[:, :head_size]
    pair_sums = weight_sums[:, head_size:]
    for level in reversed(range(group_bits)):
        half_rows = pair_sums.shape[0] // 2
        lower_half = pair_sums[:half_rows]
        upper_half = pair_sums[half_rows:]
        upper = position >> level & 1 == 1
        kept = jnp.where(upper, upper_half, lower_half)
        outgoing = jnp.where(upper, lower_half, upper_half)
        pair_sums = kept + swapped(outgoing, "seq", level)
    k_weight_grad = pair_sums[None]
    return (input_grad, attn_grad, q_weight_grad, k_weight_grad, o_weight_grad)


def solution(mesh):
    return jax.shard_map(
        shards,
        mesh=mesh,
        in_specs=(
            P("seq", ("row", "col")),
            P(("row", "col"), "seq"),
            P("seq", ("row", "col")),
            P(("row", "col"), "seq"),
            P(("row", "col"), "seq"),
            P(("row", "col"), "seq"),
            P("seq", ("row", "col"), None),
            P("seq", ("row", "col")),
        ),
        out_specs=(
            P("seq", ("row", "col")),
            P(("row", "col"), "seq"),
            P(("row", "col"), "seq"),
            P("seq", ("row", "col"), None),
            P("seq", ("row", "col")),
        ),
        check_vma=False,
    )
```

profile of v0, /device:TPU:2, one launch (start us, length us, event | category | flops | bytes accessed | tf_op | source)
XLA Modules:
  0.0 1273.0 jit_solution(12941134424129928394)
XLA Ops:
  7.2 0.7 all-gather.10.cloned.1.call-update
  8.0 0.7 all-gather.6.cloned.1.call-update
  8.7 0.7 all-gather.8.cloned.1.call-update
  10.6 158.7 %all-gather.10.cloned.1.call-done = bf16[8192,1024]{1,0:T(8,128)(2,1)} async-done(((bf16[128,1024]{1,0:T(8,128)(2,1)}), bf16[8192,1024]{1,0:T(8,128)(2,1)}) %all-gather.10.cloned.1.call-update) | async-done | bytes 16777232 | tf_op jit(solution)/shard_map/all_gather | solution.py:33
  169.3 10.1 fusion.5
  179.5 0.7 copy-done.3
  180.2 2.9 collective-permute-start
  183.1 2.1 collective-permute-done
  185.2 17.4 %collective-permute-start.1 = (bf16[256,128]{1,0:T(8,128)(2,1)S(1)}, bf16[256,128]{1,0:T(8,128)(2,1)S(1)}, u32[]{:S(2)}, u32[]{:S(2)}) collective-permute-start(bf16[256,128]{1,0:T(8,128)(2,1)S(1)} %maximum_select_fusion.2), channel_id=1, source_target_pairs={{0,8},{4,12},{8,0},{12,4},{16,24},{20,28},{24,16},{28,20},{32,40},... | collective-permute-start | bytes 196616 | tf_op jit(solution)/shard_map/ppermute | solution.py:10
  202.6 4.0 collective-permute-done.1
  206.6 4.5 collective-permute-start.2
  211.1 2.9 collective-permute-done.2
  214.1 4.6 all-gather.6.cloned.1.call-done
  218.7 3.1 constant_dynamic-update-slice_fusion.1
  221.8 30.8 %all-gather.8.cloned.1.call-done = bf16[8192,128]{1,0:T(8,128)(2,1)} async-done(((bf16[2048,128]{1,0:T(8,128)(2,1)}), bf16[8192,128]{1,0:T(8,128)(2,1)}) %all-gather.8.cloned.1.call-update) | async-done | bytes 2097168 | tf_op jit(solution)/shard_map/all_gather | solution.py:17
  252.6 3.1 constant_dynamic-update-slice_fusion
  255.8 15.7 %fusion = f32[8192,1024]{1,0:T(8,128)} fusion(bf16[8192,256]{1,0:T(8,128)(2,1)} %constant_dynamic-update-slice_fusion, bf16[1024,128]{1,0:T(8,128)(2,1)S(1)} %maximum_select_fusion, bf16[1024,128]{1,0:T(8,128)(2,1)S(1)} %copy-done.2), kind=kOutput, calls=%fused_computation.1 | convolution fusion | flops 4296015872 | bytes 38273024 | tf_op jit(solution)/shard_map/dot_general | solution.py:53
  271.4 139.9 %all-gather.12.cloned.1.call-done = bf16[8192,1024]{1,0:T(8,128)(2,1)} async-done(((bf16[128,1024]{1,0:T(8,128)(2,1)}), bf16[8192,1024]{1,0:T(8,128)(2,1)}) %all-gather.12.cloned.1.call-update) | async-done | bytes 16777232 | tf_op jit(solution)/shard_map/all_gather | solution.py:45
  411.3 9.4 convolution_bitcast_fusion
  420.7 6.6 collective-permute-start.3
  427.4 5.5 collective-permute-done.3
  433.0 13.3 %collective-permute-start.4 = (f32[256,128]{0,1:T(8,128)S(1)}, f32[256,128]{0,1:T(8,128)S(1)}, u32[]{:S(2)}, u32[]{:S(2)}) collective-permute-start(f32[256,128]{0,1:T(8,128)S(1)} %slice_select_fusion.1), channel_id=1, source_target_pairs={{0,8},{4,12},{8,0},{12,4},{16,24},{20,28},{24,16},{28,20},{32,40},... | collective-permute-start | bytes 393224 | tf_op jit(solution)/shard_map/ppermute | solution.py:10
  446.3 7.2 collective-permute-done.4
  453.6 6.0 collective-permute-start.5
  459.6 5.1 all-gather.14.cloned.1.call-done
  464.8 9.6 fusion.6
  474.4 1.0 copy.13
  475.4 0.7 copy.14
  476.2 39.5 %reduce-scatter.5.cloned.1.call-done = f32[2048,128]{1,0:T(8,128)} async-done(((f32[8192,128]{1,0:T(8,128)}), f32[2048,128]{1,0:T(8,128)}) %reduce-scatter.5.cloned.1.call-update) | async-done | bytes 1048592 | tf_op jit(solution)/shard_map/reduce_scatter | solution.py:61
  515.6 2.1 convert_element_type.7
  517.7 746.7 %reduce-scatter.3.cloned.1.call-done = f32[128,1024]{1,0:T(8,128)} async-done(((f32[8192,1024]{1,0:T(8,128)}), f32[128,1024]{1,0:T(8,128)}) %reduce-scatter.3.cloned.1.call-update) | async-done | bytes 524304 | tf_op jit(solution)/shard_map/reduce_scatter | solution.py:52
  1264.4 1.8 convert_element_type.6
  (29 shorter events, 1.7 us)
Async XLA Ops:
  7.2 162.2 %copy-start = (bf16[128,1024]{1,0:T(8,128)(2,1)S(1)}, bf16[128,1024]{1,0:T(8,128)(2,1)}, u32[]{:S(2)}) copy-start(bf16[128,1024]{1,0:T(8,128)(2,1)} %param.15) | copy-start | bytes 786436
  7.2 162.1 %all-gather.10.cloned.1.call-start = ((), (), s32[]{:S(2)}) async-start(), calls=%async_computation.5 | async-start | bytes 17039360 | tf_op jit(solution)/shard_map/all_gather | solution.py:33
  7.9 210.8 %all-gather.6.cloned.1.call-start = ((), (), s32[]{:S(2)}) async-start(), calls=%async_computation.2 | async-start | bytes 2621440 | tf_op jit(solution)/shard_map/all_gather | solution.py:16
  8.7 243.9 %all-gather.8.cloned.1.call-start = ((), (), s32[]{:S(2)}) async-start(), calls=%async_computation.3 | async-start | bytes 2621440 | tf_op jit(solution)/shard_map/all_gather | solution.py:17
  9.4 401.9 %all-gather.12.cloned.1.call-start = ((), (), s32[]{:S(2)}) async-start(), calls=%async_computation.7 | async-start | bytes 17039360 | tf_op jit(solution)/shard_map/all_gather | solution.py:45
  10.0 454.8 %all-gather.14.cloned.1.call-start = ((), (), s32[]{:S(2)}) async-start(), calls=%async_computation.8 | async-start | bytes 2621440 | tf_op jit(solution)/shard_map/all_gather | solution.py:15
  10.6 505.1 %reduce-scatter.5.cloned.1.call-start = ((), (), s32[]{:S(2)}) async-start(), calls=%async_computation.6 | async-start | bytes 5242880 | tf_op jit(solution)/shard_map/reduce_scatter | solution.py:61
  179.4 0.8 copy-start.3
  179.5 1084.9 %reduce-scatter.3.cloned.1.call-start = ((), (), s32[]{:S(2)}) async-start(), calls=%async_computation.4 | async-start | bytes 34078720 | tf_op jit(solution)/shard_map/reduce_scatter | solution.py:52
  180.2 5.0 collective-permute-start
  185.2 21.4 %collective-permute-start.1 = (bf16[256,128]{1,0:T(8,128)(2,1)S(1)}, bf16[256,128]{1,0:T(8,128)(2,1)S(1)}, u32[]{:S(2)}, u32[]{:S(2)}) collective-permute-start(bf16[256,128]{1,0:T(8,128)(2,1)S(1)} %maximum_select_fusion.2), channel_id=1, source_target_pairs={{0,8},{4,12},{8,0},{12,4},{16,24},{20,28},{24,16},{28,20},{32,40},... | collective-permute-start | bytes 196616 | tf_op jit(solution)/shard_map/ppermute | solution.py:10
  206.6 7.4 collective-permute-start.2
  214.1 41.7 %copy-start.2 = (bf16[1024,128]{1,0:T(8,128)(2,1)S(1)}, bf16[1024,128]{1,0:T(8,128)(2,1)}, u32[]{:S(2)}) copy-start(bf16[1024,128]{1,0:T(8,128)(2,1)} %param.13) | copy-start | bytes 786436
  420.7 12.2 collective-permute-start.3
  433.0 20.6 %collective-permute-start.4 = (f32[256,128]{0,1:T(8,128)S(1)}, f32[256,128]{0,1:T(8,128)S(1)}, u32[]{:S(2)}, u32[]{:S(2)}) collective-permute-start(f32[256,128]{0,1:T(8,128)S(1)} %slice_select_fusion.1), channel_id=1, source_target_pairs={{0,8},{4,12},{8,0},{12,4},{16,24},{20,28},{24,16},{28,20},{32,40},... | collective-permute-start | bytes 393224 | tf_op jit(solution)/shard_map/ppermute | solution.py:10
  453.6 21.8 %collective-permute-start.5 = (f32[128,128]{0,1:T(8,128)S(1)}, f32[128,128]{0,1:T(8,128)S(1)}, u32[]{:S(2)}, u32[]{:S(2)}) collective-permute-start(f32[128,128]{0,1:T(8,128)S(1)} %slice_select_fusion.2), channel_id=1, source_target_pairs={{0,4},{4,0},{8,12},{12,8},{16,20},{20,16},{24,28},{28,24},{32,36},... | collective-permute-start | bytes 196616 | tf_op jit(solution)/shard_map/ppermute | solution.py:10
  464.8 801.4 %copy-start.1 = (bf16[128,1024]{1,0:T(8,128)(2,1)S(1)}, bf16[128,1024]{1,0:T(8,128)(2,1)}, u32[]{:S(2)}) copy-start(bf16[128,1024]{1,0:T(8,128)(2,1)} %param.15) | copy-start | bytes 786436
Sparse Core Ops, SparseCore 0:
  11.3 157.9 all-gather.9
  171.1 47.5 all-gather.5
  220.6 32.0 all-gather.7
  255.8 155.4 all-gather.11
  413.0 51.7 all-gather.13
  467.2 48.4 reduce-scatter.4
  518.4 745.9 reduce-scatter.2
where the time goes:
time: 1280 us; the launch traced here: 1270 us
  waiting for transfers between devices  1150 us (90%)
  starting transfers between devices  51.1 us (4%)
  matrix products  44.7 us (3%)
  between operations  14.2 us (1%)
    reduce_scatter x1, waiting for transfers between devices, shards(): lax.psum_scatter(lax.dot_general(used, weight_cat, (((1,), (1,)), ((), ()...  747 us
    all_gather x1, waiting for transfers between devices, shards(): portion = lax.all_gather(out_grad, 'seq', axis=0, tiled=True)  159 us
    all_gather x1, waiting for transfers between devices, shards(): lax.all_gather(layer_input, 'seq', axis=0, tiled=True)  140 us
    ppermute x6, starting transfers between devices, swapped(): lax.ppermute(value, axis, [(i, i ^ 1 << stride) for i in range(lax.axis_s...  50.8 us
    reduce_scatter x1, waiting for transfers between devices, shards(): lax.psum_scatter(attn_part, ('row', 'col'), scatter_dimension=0, tiled=True)  39.5 us
    all_gather x1, waiting for transfers between devices, shards(): lax.all_gather(k_grad, ('row', 'col'), axis=0, tiled=True)  30.8 us
  transfers between devices with their start and end apart: 13, of which 12 were waited for; matrix products, arithmetic and copies ran while one was open for 4% of the time, Pallas kernels for 0%

commit v1 on v0

v1 whole, which is shorter than its diff:
```python
import jax
import jax.numpy as jnp
from jax import lax
from jax.experimental import pallas as pl
from jax.experimental.pallas import tpu as pltpu
from jax.sharding import PartitionSpec as P

MESH = pl.DeviceIdType.MESH
COPIES = 160
F32 = jnp.float32
BF16 = jnp.bfloat16


def rem(value, size):
    return lax.rem(value + size, size)


def at128(index):
    return pl.ds(pl.multiple_of(index * 128, 128), 128)


def at1024(index):
    return pl.ds(pl.multiple_of(index * 1024, 1024), 1024)


def kernel(
    li, ao, og, q, k, qw, kw, ow,
    ig_out, ag_out, qwg_out, kwg_out, owg_out,
    lit, ogt, qkt, aot, w3, w1, km, kbuf,
    ig, iga, igb, iga2, igb2,
    qwg, owg, kwg, qwr, owr, kwr, kwy,
    ag, agr, agb, fin,
    ssem, rsem, lsem,
):
    seq = lax.axis_index("seq")
    x, y, zh = lax.div(seq, 16), lax.rem(lax.div(seq, 4), 4), lax.rem(seq, 4)
    zlo, col = lax.axis_index("row"), lax.axis_index("col")
    z = zh * 2 + zlo
    ylo = lax.rem(y, 2)
    quarter = zlo * 2 + col

    def device(dx, dy, dz, other=False):
        zz = rem(z + dz, 8)
        return (
            rem(x + dx, 4) * 16 + rem(y + dy, 4) * 4 + lax.div(zz, 2),
            lax.rem(zz, 2),
            1 - col if other else col,
        )

    xs = [device(d, 0, 0) for d in (1, 2, 3)]
    ys = [device(0, d, 0) for d in (1, 2, 3)]
    zs = [device(0, 0, d) for d in range(1, 8)]
    sibling = device(0, 0, 0, True)
    zpartner = device(0, 0, 1 - 2 * zlo)
    ypartner = device(0, 1 - 2 * ylo, 0)
    left, right = device(0, 0, -1), device(0, 0, 1)

    barrier = pltpu.get_barrier_semaphore()
    peers = xs + ys + zs + [sibling]
    for peer in peers:
        pl.semaphore_signal(barrier, inc=1, device_id=peer, device_id_type=MESH)
    pl.semaphore_wait(barrier, len(peers))

    sent, local = [], []

    def send(src, dst, to):
        n = len(sent)
        copy = pltpu.make_async_remote_copy(
            src_ref=src, dst_ref=dst, send_sem=ssem.at[n], recv_sem=rsem.at[n],
            device_id=to, device_id_type=MESH,
        )
        copy.start()
        sent.append(copy)
        return copy

    def place(src, dst):
        copy = pltpu.make_async_copy(src, dst, lsem.at[len(local)])
        copy.start()
        local.append(copy)
        return copy

    def arrive(copies):
        for copy in copies:
            copy.wait_recv()

    def settle(copies):
        for copy in copies:
            copy.wait()

    def regroup(src, tile):
        mine = place(src.at[zlo], tile.at[x, y, :, at1024(zlo)])
        return mine, send(src.at[1 - zlo], tile.at[x, y, :, at1024(zlo)], zpartner)

    def gather_first(tile, parts):
        parts[0].wait()
        parts[1].wait_recv()
        a, b = tile.at[x, y, pl.ds(0, 32)], tile.at[x, y, pl.ds(32, 32)]
        return [send(a, a, to) for to in xs], [send(b, b, to) for to in ys]

    def gather_second(tile, parts):
        arrive(parts[0])
        a = tile.at[:, y, pl.ds(0, 32)]
        first = [send(a, a, to) for to in ys]
        arrive(parts[1])
        b = tile.at[x, :, pl.ds(32, 32)]
        return first + [send(b, b, to) for to in xs]

    def spread(src, slot):
        copies = [
            send(src.at[:, rem(z + d, 8)], slot(zh, zlo), zs[d - 1]) for d in range(1, 8)
        ]
        return place(src.at[:, z], slot(zh, zlo)), copies

    def ring_gather(piece):
        own = piece(z, None)
        steps = [[send(own, own, left), send(own, own, right)]]

        def step(s):
            arrive(steps[-1])
            half = s == 4
            a = piece(rem(z + s - 1, 8), 0 if half else None)
            b = piece(rem(z - s + 1, 8), 1 if half else None)
            steps.append([send(a, a, left), send(b, b, right)])

        return step, lambda: arrive(steps[-1])

    def ring_reduce(piece, got, half_rows):
        far = rem(z + 4, 8)
        h0, h1 = pl.ds(0, half_rows), pl.ds(half_rows, half_rows)
        steps = [[
            send(piece(far).at[h0], got.at[0, 0, h0], left),
            send(piece(far).at[h1], got.at[1, 0, h1], right),
        ]]

        def step(s):
            arrive(steps[-1])
            a, b = piece(rem(z - (5 - s), 8)), piece(rem(z + (5 - s), 8))
            if s == 2:
                a[h0] = a[h0] + got[0, 0, h0]
                b[h1] = b[h1] + got[1, 0, h1]
            else:
                a[...] = a[...] + got[0, s - 2]
                b[...] = b[...] + got[1, s - 2]
            steps.append([
                send(a, got.at[0, s - 1], left), send(b, got.at[1, s - 1], right)
            ])

        def total():
            arrive(steps[-1])
            return piece(z)[...] + got[0, 3] + got[1, 3]

        return step, total

    def qw_slot(zz, half):
        rows = pl.ds(0, 1024) if half is None else pl.ds(half * 512, 512)
        return w3.at[lax.rem(zz, 2), rows, at128(lax.div(zz, 2))]

    def km_slot(zz, half):
        pairs = pl.ds(0, 2) if half is None else pl.ds(half, 1)
        return km.at[lax.rem(zz, 2), pairs, lax.div(zz, 2)]

    def ow_slot(zz, half):
        rows = pl.ds(0, 128) if half is None else pl.ds(half * 64, 64)
        return w1.at[lax.div(zz, 2), rows, at1024(lax.rem(zz, 2))]


    li_parts = regroup(li, lit)
    og_parts = regroup(og, ogt)
    km_own = place(kw, km.at[zlo, ylo, zh])
    km_sent = send(kw, km.at[zlo, ylo, zh], ypartner)
    qw_own = place(qw, qw_slot(z, None))
    ow_own = place(ow, ow_slot(z, None))

    def head_slot(tile):
        return lambda h, lo: tile.at[quarter, :, :, at128(h)]

    q_own, q_copies = spread(q, head_slot(qkt))
    k_own, k_copies = spread(k, lambda h, lo: kbuf.at[h, lo])
    qw_own.wait()
    qw_step, qw_done = ring_gather(qw_slot)
    li_first = gather_first(lit, li_parts)
    og_first = gather_first(ogt, og_parts)
    km_own.wait()
    km_sent.wait_recv()
    km_step, km_done = ring_gather(km_slot)
    ao_own, ao_copies = spread(ao, head_slot(aot))
    qw_step(2)
    km_step(2)
    li_second = gather_second(lit, li_first)
    qw_step(3)
    km_step(3)
    og_second = gather_second(ogt, og_first)
    ow_own.wait()
    ow_step, ow_done = ring_gather(ow_slot)
    qw_step(4)
    km_step(4)

    k_own.wait()
    arrive(k_copies)

    for lo in range(2):
        total = kbuf[0, lo].astype(F32)
        for h in range(1, 4):
            total = total + kbuf[h, lo].astype(F32)
        high = total.astype(BF16)
        qkt[lo * 2 + col, :, :, pl.ds(512, 128)] = high
        qkt[lo * 2 + col, :, :, pl.ds(640, 128)] = (total - high.astype(F32)).astype(BF16)
    q_own.wait()
    arrive(q_copies)

    def exchange(tile):
        views = [tile.at[lo * 2 + col] for lo in range(2)]
        return [send(view, view, sibling) for view in views]

    q_shared = exchange(qkt)
    ow_step(2)
    arrive(li_second)
    arrive(q_shared)

    for lo in range(2):
        def block(i, _, lo=lo):
            cols = pl.ds(pl.multiple_of(lo * 1024 + i * 256, 256), 256)
            rows = pl.ds(pl.multiple_of(i * 256, 256), 256)
            part = lax.dot_general(
                lit[:, :, :, cols].reshape(1024, 256), qkt[...].reshape(1024, 768),
                (((0,), (0,)), ((), ())), preferred_element_type=F32,
            )
            for h in range(4):
                qwg[lo, h, rows, :] = part[:, h * 128 : h * 128 + 128]
            sums = part[:, 512:640] + part[:, 640:768]
            kwg[lo, lax.div(i, 2), pl.ds(lax.rem(i, 2) * 2, 2)] = sums.reshape(2, 128, 128)
            return 0
        lax.fori_loop(0, 4, block, 0)
    kwg_sent = send(kwg.at[:, 1 - ylo], kwy, ypartner)
    qwg_step, qwg_total = ring_reduce(
        lambda zz: qwg.at[lax.rem(zz, 2), lax.div(zz, 2)], qwr, 512
    )

    qw_done()
    km_done()
    for lo in range(2):
        keys = km[lo].reshape(1024, 128)
        w3[lo, :, pl.ds(512, 128)] = keys
        w3[lo, :, pl.ds(640, 128)] = keys
    for lo in range(2):
        def block(i, _, lo=lo):
            cols = pl.ds(pl.multiple_of(lo * 1024 + i * 256, 256), 256)
            rows = pl.ds(pl.multiple_of(i * 256, 256), 256)
            part = lax.dot_general(
                qkt[...].reshape(1024, 768), w3[lo, rows, :],
                (((1,), (1,)), ((), ())), preferred_element_type=F32,
            )
            ig[:, :, :, cols] = part.reshape(4, 4, 64, 256)
            return 0
        lax.fori_loop(0, 4, block, 0)
    a_rows, b_rows = pl.ds(0, 32), pl.ds(32, 32)
    ig_first = [
        send(ig.at[:, rem(y + d, 4), a_rows], iga.at[d - 1], ys[d - 1]) for d in (1, 2, 3)
    ] + [
        send(ig.at[rem(x + d, 4), :, b_rows], igb.at[d - 1], xs[d - 1]) for d in (1, 2, 3)
    ]
    ow_step(3)

    ao_own.wait()
    arrive(ao_copies)
    ao_shared = exchange(aot)
    arrive(og_second)
    arrive(ao_shared)
    for lo in range(2):
        def block(i, _, lo=lo):
            cols = pl.ds(pl.multiple_of(lo * 1024 + i * 512, 512), 512)
            part = lax.dot_general(
                aot[...].reshape(1024, 512), ogt[:, :, :, cols].reshape(1024, 512),
                (((0,), (0,)), ((), ())), preferred_element_type=F32,
            )
            owg[:, lo, :, pl.ds(pl.multiple_of(i * 512, 512), 512)] = part.reshape(4, 128, 512)
            return 0
        lax.fori_loop(0, 2, block, 0)
    owg_step, owg_total = ring_reduce(
        lambda zz: owg.at[lax.div(zz, 2), lax.rem(zz, 2)], owr, 64
    )
    ow_step(4)
    kwg_sent.wait()
    kwg[:, ylo] = kwg[:, ylo] + kwy[...]
    kwg_step, kwg_total = ring_reduce(
        lambda zz: kwg.at[lax.rem(zz, 2), ylo, lax.div(zz, 2)], kwr, 64
    )
    qwg_step(2)
    owg_step(2)
    kwg_step(2)

    ow_done()

    def block(i, _):
        part = lax.dot_general(
            ogt[i].reshape(256, 2048), w1[...].reshape(512, 2048),
            (((1,), (1,)), ((), ())), preferred_element_type=F32,
        )
        ag[i] = part.reshape(4, 64, 512)
        return 0

    lax.fori_loop(0, 4, block, 0)
    ag_sent = [send(ag.at[lo * 2 + 1 - col], agr.at[lo], sibling) for lo in range(2)]
    for lo in range(2):
        ag_sent[lo].wait_recv()
        agb[lo] = (ag[lo * 2 + col] + agr[lo]).astype(BF16)
    ag_own = place(agb.at[zlo, :, :, at128(zh)], ag_out.at[:, z])
    ag_copies = []
    for d in range(1, 8):
        zz = rem(z + d, 8)
        ag_copies.append(send(
            agb.at[lax.rem(zz, 2), :, :, at128(lax.div(zz, 2))], ag_out.at[:, z], zs[d - 1]
        ))

    arrive(ig_first)

    def add_a(i, _):
        ig[i, y, a_rows] = ig[i, y, a_rows] + iga[0, i] + iga[1, i] + iga[2, i]
        return 0

    def add_b(i, _):
        ig[x, i, b_rows] = ig[x, i, b_rows] + igb[0, i] + igb[1, i] + igb[2, i]
        return 0

    lax.fori_loop(0, 4, add_a, 0)
    lax.fori_loop(0, 4, add_b, 0)
    ig_second = [
        send(ig.at[rem(x + d, 4), y, a_rows], iga2.at[d - 1], xs[d - 1]) for d in (1, 2, 3)
    ] + [
        send(ig.at[x, rem(y + d, 4), b_rows], igb2.at[d - 1], ys[d - 1]) for d in (1, 2, 3)
    ]
    qwg_step(3)
    owg_step(3)
    kwg_step(3)
    arrive(ig_second)
    fin[pl.ds(0, 32), :] = (ig[x, y, a_rows] + iga2[0] + iga2[1] + iga2[2]).astype(BF16)
    fin[pl.ds(32, 32), :] = (ig[x, y, b_rows] + igb2[0] + igb2[1] + igb2[2]).astype(BF16)
    ig_own = place(fin.at[:, at1024(zlo)], ig_out.at[zlo])
    ig_sent = send(fin.at[:, at1024(1 - zlo)], ig_out.at[zlo], zpartner)
    qwg_step(4)
    owg_step(4)
    kwg_step(4)
    qwg_out[...] = qwg_total()
    kwg_out[...] = kwg_total()
    owg_out[...] = owg_total()
    arrive(ag_copies)
    ag_own.wait()
    ig_sent.wait_recv()
    ig_own.wait()
    for copy in sent:
        if copy is not kwg_sent:
            copy.wait_send()


def shards(layer_input, attn_out, out_grad, q_grad, k_grad, q_weight, k_weight, o_weight):
    shapes = (
        ((2, 64, 1024), BF16), ((4, 8, 64, 128), BF16), ((1024, 128), F32),
        ((128, 128), F32), ((128, 1024), F32),
    )
    vmem = pltpu.VMEM
    scratch = [
        vmem((4, 4, 64, 2048), BF16),
        vmem((4, 4, 64, 2048), BF16),
        vmem((4, 4, 64, 768), BF16),
        vmem((4, 4, 64, 512), BF16),
        vmem((2, 1024, 768), BF16),
        vmem((4, 128, 2048), BF16),
        vmem((2, 2, 4, 128, 128), BF16),
        vmem((4, 2, 4, 64, 128), BF16),
        vmem((4, 4, 64, 2048), F32),
        vmem((3, 4, 32, 2048), F32),
        vmem((3, 4, 32, 2048), F32),
        vmem((3, 32, 2048), F32),
        vmem((3, 32, 2048), F32),
        vmem((2, 4, 1024, 128), F32),
        vmem((4, 2, 128, 1024), F32),
        vmem((2, 2, 4, 128, 128), F32),
        vmem((2, 4, 1024, 128), F32),
        vmem((2, 4, 128, 1024), F32),
        vmem((2, 4, 128, 128), F32),
        vmem((2, 4, 128, 128), F32),
        vmem((4, 4, 64, 512), F32),
        vmem((2, 4, 64, 512), F32),
        vmem((2, 4, 64, 512), BF16),
        vmem((64, 2048), BF16),
        pltpu.SemaphoreType.DMA((COPIES,)),
        pltpu.SemaphoreType.DMA((COPIES,)),
        pltpu.SemaphoreType.DMA((16,)),
    ]
    ig, ag, qwg, kwg, owg = pl.pallas_call(
        kernel,
        out_shape=[jax.ShapeDtypeStruct(*shape) for shape in shapes],
        in_specs=[pl.BlockSpec(memory_space=pl.ANY)] * 8,
        out_specs=[pl.BlockSpec(memory_space=pltpu.VMEM)] * 5,
        scratch_shapes=scratch,
        compiler_params=pltpu.CompilerParams(
            collective_id=0, has_side_effects=True, vmem_limit_bytes=62 * 2**20
        ),
        cost_estimate=pl.CostEstimate(flops=14 * 10**9, bytes_accessed=5 * 10**6, transcendentals=0),
    )(
        layer_input.reshape(2, 64, 1024),
        attn_out.reshape(4, 8, 64, 128),
        out_grad.reshape(2, 64, 1024),
        q_grad.reshape(4, 8, 64, 128),
        k_grad.reshape(4, 8, 64, 128),
        q_weight,
        k_weight[0],
        o_weight,
    )
    return (
        ig.reshape(128, 1024),
        ag.reshape(2048, 128),
        qwg,
        kwg[None],
        owg,
    )


def solution(mesh):
    return jax.shard_map(
        shards,
        mesh=mesh,
        in_specs=(
            P("seq", ("row", "col")),
            P(("row", "col"), "seq"),
            P("seq", ("row", "col")),
            P(("row", "col"), "seq"),
            P(("row", "col"), "seq"),
            P(("row", "col"), "seq"),
            P("seq", ("row", "col"), None),
            P("seq", ("row", "col")),
        ),
        out_specs=(
            P("seq", ("row", "col")),
            P(("row", "col"), "seq"),
            P(("row", "col"), "seq"),
            P("seq", ("row", "col"), None),
            P("seq", ("row", "col")),
        ),
        check_vma=False,
    )
```

time: 1280 us -> 213 us (0.17)
  waiting for transfers between devices: 1150 us -> 0 us
  Pallas kernels: 0 us -> 207 us
  starting transfers between devices: 51.1 us -> 0 us
  matrix products: 44.7 us -> 0 us
  between operations: 14.2 us -> 0.66 us
    reduce_scatter x2 -> x0, waiting for transfers between devices: 786 us -> none  [the longest x1 747 us: shards(): lax.psum_scatter(lax.dot_general(used, weight_cat, (((1,), (1,)), ((), ()...]
    all_gather x5 -> x0, waiting for transfers between devices: 339 us -> none  [the longest x1 159 us: shards(): portion = lax.all_gather(out_grad, 'seq', axis=0, tiled=True)]
    pallas_call x0 -> x1, Pallas kernels: none -> 207 us  [shards(): pl.pallas_call(kernel, out_shape=[jax.ShapeDtypeStruct(*shape) for shape...]
    ppermute x6 -> x0, starting transfers between devices: 50.8 us -> none  [swapped(): lax.ppermute(value, axis, [(i, i ^ 1 << stride) for i in range(lax.axis_s...]
    dot_general x4 -> x0, matrix products: 44.7 us -> none  [the longest x1 15.7 us: shards(): lax.dot_general(used, weight_cat, (((1,), (1,)), ((), ())), preferred_ele...]
    ppermute x6 -> x0, waiting for transfers between devices: 21.7 us -> none  [swapped(): lax.ppermute(value, axis, [(i, i ^ 1 << stride) for i in range(lax.axis_s...]
  transfers between devices with their start and end apart: 13 -> 0, of which waited for: 12 -> 0; matrix products, arithmetic and copies ran while one was open for 4% -> 0% of each run, Pallas kernels for 0% -> 0%
where the time goes in v1:
time: 213 us
  Pallas kernels  207 us (97%)
  local copies, waits for them, and re-layouts  5.25 us (2%)
    pallas_call x1, Pallas kernels, shards(): pl.pallas_call(kernel, out_shape=[jax.ShapeDtypeStruct(*shape) for shape...  207 us
    unnamed x13, local copies, waits for them, and re-layouts  5.25 us

profile of v1, /device:TPU:2, one launch (start us, length us, event | category | flops | bytes accessed | tf_op | source)
XLA Modules:
  0.0 212.5 jit_solution(4520392629038484303)
XLA Ops:
  0.6 206.6 %shard_map.119 = (bf16[2,64,1024]{2,1,0:T(8,128)(2,1)}, bf16[4,8,64,128]{3,2,1,0:T(8,128)(2,1)}, f32[1024,128]{1,0:T(8,128)}, f32[128,128]{1,0:T(8,128)}, f32[128,1024]{1,0:T(8,128)}) custom-call(bf16[2,64,1024]{2,1,0:T(8,128)(2,1)} %bitcast.15, bf16[4,8,64,128]{3,2,1,0:T(8,128)(2,1)} %bitcast.12, bf16[2,64,1024]{2,1,0:T(8,128)(2,1)} %bitcast.16, ...), custom_call_target="tpu_custom_call" | custom-call | flops 14000000000 | bytes 5000000 | tf_op jit(solution)/shard_map/pallas_call | solution.py:390
  207.3 0.0 copy-start.2
  207.3 1.7 copy.18
  209.0 0.0 copy-done.2
  209.0 0.0 copy-start.1
  209.0 0.8 copy.19
  209.8 0.4 copy-done.1
  210.2 0.0 copy-start.3
  210.2 0.0 copy-start
  210.2 0.8 copy.20
  211.0 0.1 copy-done.3
  211.1 0.6 copy.21
  211.7 0.0 copy-done
  211.7 0.8 copy.22
Async XLA Ops:
  207.3 1.7 copy-start.2
  209.0 1.2 copy-start.1
  210.2 0.9 copy-start.3
  210.2 1.5 copy-start

commit v2 on v1

v2 whole, which is shorter than its diff:
```python
import jax
import jax.numpy as jnp
from jax import lax
from jax.experimental import pallas as pl
from jax.experimental.pallas import tpu as pltpu
from jax.sharding import PartitionSpec as P

MESH = pl.DeviceIdType.MESH
COPIES = 160
F32 = jnp.float32
BF16 = jnp.bfloat16


def rem(value, size):
    return lax.rem(value + size, size)


def at128(index):
    return pl.ds(pl.multiple_of(index * 128, 128), 128)


def at1024(index):
    return pl.ds(pl.multiple_of(index * 1024, 1024), 1024)


def kernel(
    li, ao, og, q, k, qw, kw, ow,
    ig_out, ag_out, qwg_out, kwg_out, owg_out,
    lit, owt, ogt, qkt, aot, w3, km, kbuf,
    ig, owg, ig_got, owg_got,
    qwg, kwg, qw_far, qw_full, kw_far, kw_full, kwy,
    agr, agb, fin,
    ssem, rsem, lsem, gsem,
):
    seq = lax.axis_index("seq")
    x, y, zh = lax.div(seq, 16), lax.rem(lax.div(seq, 4), 4), lax.rem(seq, 4)
    zlo, col = lax.axis_index("row"), lax.axis_index("col")
    z = zh * 2 + zlo
    yhi, ylo = lax.div(y, 2), lax.rem(y, 2)
    quarter = zlo * 2 + col

    def at(xx, yy, lo, core):
        return (xx * 16 + yy * 4 + zh, lo, core)

    def device(dx, dy, dz):
        zz = rem(z + dz, 8)
        return (
            rem(x + dx, 4) * 16 + rem(y + dy, 4) * 4 + lax.div(zz, 2), lax.rem(zz, 2), col
        )

    zs = [device(0, 0, d) for d in range(1, 8)]
    sibling = at(x, y, zlo, 1 - col)
    zpartner = device(0, 0, 1 - 2 * zlo)
    ypartner = device(0, 1 - 2 * ylo, 0)
    x_ring = (4, x, device(-1, 0, 0), device(1, 0, 0))
    y_ring = (4, y, device(0, -1, 0), device(0, 1, 0))
    z_ring = (8, z, device(0, 0, -1), device(0, 0, 1))

    square = ylo == zlo
    home = jnp.logical_and(x == quarter, y == col * 2 + zlo)
    spread_ow = [(at(x, yhi * 2 + r, ylo, col), jnp.logical_and(square, ylo == r)) for r in range(2)]
    return_ow = [(at(x, yhi * 2 + zlo, b, col), jnp.logical_and(square, zlo == b)) for b in range(2)]
    spread_ao = [(at(quarter, j, ylo, yhi), jnp.logical_and(home, y == j)) for j in range(4)]
    return_ag = [
        (at(i, col * 2 + zlo, lax.div(x, 2), lax.rem(x, 2)), jnp.logical_and(home, x == i))
        for i in range(4)
    ]

    barrier = pltpu.get_barrier_semaphore()
    peers = list(x_ring[2:]) + list(y_ring[2:]) + zs + [sibling]
    for peer in peers:
        pl.semaphore_signal(barrier, inc=1, device_id=peer, device_id_type=MESH)
    for peer, own in spread_ow + return_ow + spread_ao + return_ag:
        @pl.when(jnp.logical_not(own))
        def _(peer=peer):
            pl.semaphore_signal(barrier, inc=1, device_id=peer, device_id_type=MESH)
    count = len(peers) + 12 - 2 * square.astype(jnp.int32) - 2 * home.astype(jnp.int32)
    pl.semaphore_wait(barrier, count)

    sent, local, guarded = [], [], []

    def send(src, dst, to):
        n = len(sent)
        copy = pltpu.make_async_remote_copy(
            src_ref=src, dst_ref=dst, send_sem=ssem.at[n], recv_sem=rsem.at[n],
            device_id=to, device_id_type=MESH,
        )
        copy.start()
        sent.append(copy)
        return copy

    def place(src, dst):
        copy = pltpu.make_async_copy(src, dst, lsem.at[len(local)])
        copy.start()
        local.append(copy)
        return copy

    def post(src, dst, partner, slot):
        to, own = partner
        copy = pltpu.make_async_remote_copy(
            src_ref=src, dst_ref=dst, send_sem=gsem.at[16 + len(guarded)],
            recv_sem=gsem.at[slot], device_id=to, device_id_type=MESH,
        )

        @pl.when(jnp.logical_not(own))
        def _():
            copy.start()

        @pl.when(own)
        def _():
            pltpu.make_async_copy(src, dst, gsem.at[slot]).start()

        guarded.append((copy, own))

    def collect(dst, slot):
        pltpu.make_async_copy(dst, dst, gsem.at[slot]).wait()

    def arrive(copies):
        for copy in copies:
            copy.wait_recv()

    def add(dst, *parts):
        if len(dst.shape) == 3:
            def row(i, _):
                total = dst[i]
                for part in parts:
                    total = total + part[i]
                dst[i] = total
                return 0
            lax.fori_loop(0, dst.shape[0], row, 0)
        else:
            total = dst[...]
            for part in parts:
                total = total + part[...]
            dst[...] = total

    def ring_gather(ring, piece):
        n, me, left, right = ring
        own = piece(me, None)
        steps = [[send(own, own, left), send(own, own, right)]]

        def step(s):
            arrive(steps[-1])
            half = s == n // 2
            a = piece(rem(me + s - 1, n), 0 if half else None)
            b = piece(rem(me - s + 1, n), 1 if half else None)
            steps.append([send(a, a, left), send(b, b, right)])

        return step, lambda: arrive(steps[-1])

    def ring_reduce(ring, piece, far, full):
        n, me, left, right = ring
        size = far(0).shape[0]
        halves = [pl.ds(0, size), pl.ds(size, size)]
        last = n // 2
        across = piece(rem(me + last, n))
        steps = [[
            send(across.at[halves[0]], far(0), left), send(across.at[halves[1]], far(1), right)
        ]]

        def step(s):
            arrive(steps[-1])
            a, b = piece(rem(me - (last + 1 - s), n)), piece(rem(me + (last + 1 - s), n))
            if s == 2:
                add(a.at[halves[0]], far(0))
                add(b.at[halves[1]], far(1))
            else:
                add(a, full(0, s - 3))
                add(b, full(1, s - 3))
            steps.append([send(a, full(0, s - 2), left), send(b, full(1, s - 2), right)])

        def total():
            arrive(steps[-1])
            add(piece(me), full(0, last - 2), full(1, last - 2))
            return piece(me)

        return step, total

    def part_of(size, half):
        return pl.ds(0, size) if half is None else pl.ds(half * (size // 2), size // 2)

    def rows_of(start, half):
        return pl.ds(start, 32) if half is None else pl.ds(start + half * 16, 16)

    class Gather:
        def __init__(self, tile):
            self.tile = tile
            self.a = ring_gather(x_ring, lambda i, h: tile.at[i, y, rows_of(0, h)])
            self.b = ring_gather(y_ring, lambda j, h: tile.at[x, j, rows_of(32, h)])

        def inner(self):
            self.a[0](2)
            self.b[0](2)

        def outer(self):
            tile = self.tile
            self.a[1]()
            self.a = ring_gather(y_ring, lambda j, h: tile.at[part_of(4, h), j, pl.ds(0, 32)])
            self.b[1]()
            self.b = ring_gather(x_ring, lambda i, h: tile.at[i, part_of(4, h), pl.ds(32, 32)])

        def done(self):
            self.a[1]()
            self.b[1]()

    class Reduce:
        def __init__(self, tile, got):
            self.tile, self.got = tile, got
            far, full = got[0], got[1]
            self.a = ring_reduce(
                y_ring, lambda j: tile.at[:, j, pl.ds(0, 32)],
                lambda d: far.at[0, d], lambda d, s: full.at[0, d],
            )
            self.b = ring_reduce(
                x_ring, lambda i: tile.at[i, :, pl.ds(32, 32)],
                lambda d: far.at[1, d], lambda d, s: full.at[1, d],
            )

        def second(self):
            self.a[0](2)
            self.b[0](2)

        def inner(self):
            tile = self.tile
            far, full = self.got[2], self.got[3]
            self.a[1]()
            self.a = ring_reduce(
                x_ring, lambda i: tile.at[i, y, pl.ds(0, 32)],
                lambda d: far.at[0, d], lambda d, s: full.at[0, d],
            )
            self.b[1]()
            self.b = ring_reduce(
                y_ring, lambda j: tile.at[x, j, pl.ds(32, 32)],
                lambda d: far.at[1, d], lambda d, s: full.at[1, d],
            )

        def total(self):
            self.a[1]()
            self.b[1]()

    def spread(src, slot):
        copies = [
            send(src.at[:, rem(z + d, 8)], slot, zs[d - 1]) for d in range(1, 8)
        ]
        return place(src.at[:, z], slot), copies

    def qw_slot(zz, half):
        return w3.at[lax.rem(zz, 2), part_of(1024, half), at128(lax.div(zz, 2))]

    def km_slot(zz, half):
        return km.at[lax.rem(zz, 2), part_of(2, half), lax.div(zz, 2)]

    def og_slot(zz, half):
        return ogt.at[lax.div(zz, 2), part_of(128, half), at1024(lax.rem(zz, 2))]

    li_slot = lit.at[x, y, :, at1024(zlo)]
    li_own = place(li.at[zlo], li_slot)
    li_sent = send(li.at[1 - zlo], li_slot, zpartner)
    for r in range(2):
        post(
            ow.at[pl.ds(r * 64, 64)], owt.at[x, yhi * 2 + r, :, at1024(zlo)], spread_ow[r], zlo
        )
    km_own = place(kw, km.at[zlo, ylo, zh])
    km_sent = send(kw, km.at[zlo, ylo, zh], ypartner)
    qw_own = place(qw, qw_slot(z, None))
    og_own = place(og, og_slot(z, None))
    q_own, q_copies = spread(q, qkt.at[quarter, :, :, at128(zh)])
    qw_own.wait()
    qw_step, qw_done = ring_gather(z_ring, qw_slot)
    k_own, k_copies = spread(k, kbuf.at[zh, zlo])
    li_own.wait()
    li_sent.wait_recv()
    li_all = Gather(lit)
    for b in range(2):
        collect(owt.at[x, y, :, pl.ds(b * 1024, 1024)], b)
    ow_all = Gather(owt)
    for j in range(4):
        post(ao.at[j], aot.at[yhi, :, :, at128(x)], spread_ao[j], 2 + x)
    km_own.wait()
    km_sent.wait_recv()
    km_step, km_done = ring_gather(z_ring, km_slot)
    li_all.inner()
    ow_all.inner()
    qw_step(2)
    og_own.wait()
    og_step, og_done = ring_gather(z_ring, og_slot)
    km_step(2)
    li_all.outer()
    qw_step(3)
    km_step(3)
    ow_all.outer()
    og_step(2)
    qw_step(4)
    km_step(4)
    li_all.inner()
    og_step(3)
    ow_all.inner()

    k_own.wait()
    arrive(k_copies)
    for lo in range(2):
        total = kbuf[0, lo].astype(F32)
        for h in range(1, 4):
            total = total + kbuf[h, lo].astype(F32)
        high = total.astype(BF16)
        qkt[lo * 2 + col, :, :, pl.ds(512, 128)] = high
        qkt[lo * 2 + col, :, :, pl.ds(640, 128)] = (total - high.astype(F32)).astype(BF16)
    q_own.wait()
    arrive(q_copies)
    q_shared = [send(v, v, sibling) for v in [qkt.at[lo * 2 + col] for lo in range(2)]]

    qw_done()
    km_done()
    for lo in range(2):
        keys = km[lo].reshape(1024, 128)
        w3[lo, :, pl.ds(512, 128)] = keys
        w3[lo, :, pl.ds(640, 128)] = keys
    arrive(q_shared)
    for lo in range(2):
        def block(i, _, lo=lo):
            cols = pl.ds(pl.multiple_of(lo * 1024 + i * 256, 256), 256)
            rows = pl.ds(pl.multiple_of(i * 256, 256), 256)
            part = lax.dot_general(
                qkt[...].reshape(1024, 768), w3[lo, rows, :],
                (((1,), (1,)), ((), ())), preferred_element_type=F32,
            )
            ig[:, :, :, cols] = part.reshape(4, 4, 64, 256)
            return 0
        lax.fori_loop(0, 4, block, 0)
    ig_sum = Reduce(ig, ig_got)
    og_step(4)

    li_all.done()
    for lo in range(2):
        def block(i, _, lo=lo):
            cols = pl.ds(pl.multiple_of(lo * 1024 + i * 256, 256), 256)
            rows = pl.ds(pl.multiple_of(i * 256, 256), 256)
            part = lax.dot_general(
                lit[:, :, :, cols].reshape(1024, 256), qkt[...].reshape(1024, 768),
                (((0,), (0,)), ((), ())), preferred_element_type=F32,
            )
            for h in range(4):
                qwg[lo, h, rows, :] = part[:, h * 128 : h * 128 + 128]
            sums = part[:, 512:640] + part[:, 640:768]
            kwg[lo, lax.div(i, 2), pl.ds(lax.rem(i, 2) * 2, 2)] = sums.reshape(2, 128, 128)
            return 0
        lax.fori_loop(0, 4, block, 0)
    qwg_step, qwg_total = ring_reduce(
        z_ring, lambda zz: qwg.at[lax.rem(zz, 2), lax.div(zz, 2)],
        lambda d: qw_far.at[d], lambda d, s: qw_full.at[d, s],
    )
    kwg_step, kwg_total = ring_reduce(
        z_ring, lambda zz: kwg.at[lax.rem(zz, 2), :, lax.div(zz, 2)],
        lambda d: kw_far.at[d], lambda d, s: kw_full.at[d, s],
    )

    for i in range(4):
        collect(aot.at[col, :, :, pl.ds(i * 128, 128)], 2 + i)
    ao_shared = send(aot.at[col], aot.at[col], sibling)
    ow_all.done()
    og_done()
    for h in range(2):
        part = lax.dot_general(
            ogt[...].reshape(512, 2048), owt[:, pl.ds(2 * h, 2)].reshape(512, 2048),
            (((1,), (1,)), ((), ())), preferred_element_type=F32,
        ).reshape(4, 2, 64, 512)
        owg[h, :, :, pl.ds(0, 512)] = part[:, 0]
        owg[h, :, :, pl.ds(512, 512)] = part[:, 1]
    ag_sent = send(owg.at[1 - col, :, :, pl.ds(0, 1024)], agr, sibling)
    qwg_step(2)
    kwg_step(2)
    ag_sent.wait()
    for half in range(2):
        cols = pl.ds(half * 512, 512)
        agb[:, pl.ds(half * 64, 64), :] = (owg[col, :, :, cols] + agr[:, :, cols]).astype(BF16)

    ao_shared.wait_recv()
    for h in range(2):
        def block(i, _, h=h):
            cols = pl.ds(pl.multiple_of(i * 512, 512), 512)
            part = lax.dot_general(
                aot[h].reshape(512, 512), ogt[:, :, cols].reshape(512, 512),
                (((0,), (0,)), ((), ())), preferred_element_type=F32,
            )
            owg[:, pl.ds(2 * h, 2), :, cols] = part.reshape(4, 2, 64, 512)
            return 0
        lax.fori_loop(0, 4, block, 0)
    owg_sum = Reduce(owg, owg_got)
    for i in range(4):
        post(agb.at[:, :, pl.ds(i * 128, 128)], ag_out.at[y], return_ag[i], 6 + y)

    ig_sum.second()
    qwg_step(3)
    kwg_step(3)
    owg_sum.second()
    qwg_step(4)
    kwg_step(4)
    ig_sum.inner()
    ig_sum.second()
    kwg_mine = kwg_total()
    kwg_sent = send(kwg_mine.at[1 - ylo], kwy, ypartner)
    qwg_own = place(qwg_total(), qwg_out)
    owg_sum.inner()
    ig_sum.total()
    fin[...] = ig[x, y].astype(BF16)
    ig_own = place(fin.at[:, at1024(zlo)], ig_out.at[zlo])
    ig_sent = send(fin.at[:, at1024(1 - zlo)], ig_out.at[zlo], zpartner)
    kwg_sent.wait_recv()
    kwy[...] = kwy[...] + kwg_mine[ylo]
    kwg_own = place(kwy, kwg_out)
    owg_sum.second()
    owg_sum.total()
    for b in range(2):
        post(
            owg.at[x, y, :, pl.ds(b * 1024, 1024)],
            owg_out.at[pl.ds(pl.multiple_of(ylo * 64, 64), 64)], return_ow[b], 10 + ylo,
        )
    for copy in sent:
        if copy is not ag_sent:
            copy.wait_send()
    for copy, own in guarded:
        @pl.when(jnp.logical_not(own))
        def _(copy=copy):
            copy.wait_send()
    for j in range(4):
        collect(ag_out.at[j], 6 + j)
    for r in range(2):
        collect(owg_out.at[pl.ds(r * 64, 64)], 10 + r)
    ig_sent.wait_recv()
    for copy in (qwg_own, ig_own, kwg_own):
        copy.wait()


def shards(layer_input, attn_out, out_grad, q_grad, k_grad, q_weight, k_weight, o_weight):
    shapes = (
        ((2, 64, 1024), BF16), ((4, 4, 128, 128), BF16), ((1024, 128), F32),
        ((128, 128), F32), ((128, 1024), F32),
    )
    vmem = pltpu.VMEM
    def reduction():
        return (
            vmem((2, 2, 2, 32, 2048), F32), vmem((2, 2, 4, 32, 2048), F32),
            vmem((2, 2, 16, 2048), F32), vmem((2, 2, 32, 2048), F32),
        )

    scratch = [
        vmem((4, 4, 64, 2048), BF16),
        vmem((4, 4, 64, 2048), BF16),
        vmem((4, 128, 2048), BF16),
        vmem((4, 4, 64, 768), BF16),
        vmem((2, 4, 128, 512), BF16),
        vmem((2, 1024, 768), BF16),
        vmem((2, 2, 4, 128, 128), BF16),
        vmem((4, 2, 4, 64, 128), BF16),
        vmem((4, 4, 64, 2048), F32),
        vmem((4, 4, 64, 2048), F32),
        reduction(),
        reduction(),
        vmem((2, 4, 1024, 128), F32),
        vmem((2, 2, 4, 128, 128), F32),
        vmem((2, 512, 128), F32),
        vmem((2, 3, 1024, 128), F32),
        vmem((2, 1, 128, 128), F32),
        vmem((2, 3, 2, 128, 128), F32),
        vmem((128, 128), F32),
        vmem((4, 64, 1024), F32),
        vmem((4, 128, 512), BF16),
        vmem((64, 2048), BF16),
        pltpu.SemaphoreType.DMA((COPIES,)),
        pltpu.SemaphoreType.DMA((COPIES,)),
        pltpu.SemaphoreType.DMA((16,)),
        pltpu.SemaphoreType.DMA((32,)),
    ]
    ig, ag, qwg, kwg, owg = pl.pallas_call(
        kernel,
        out_shape=[jax.ShapeDtypeStruct(*shape) for shape in shapes],
        in_specs=[pl.BlockSpec(memory_space=pl.ANY)] * 8,
        out_specs=[pl.BlockSpec(memory_space=pl.ANY)] * 5,
        scratch_shapes=scratch,
        compiler_params=pltpu.CompilerParams(
            collective_id=0, has_side_effects=True, vmem_limit_bytes=63 * 2**20
        ),
        cost_estimate=pl.CostEstimate(flops=14 * 10**9, bytes_accessed=5 * 10**6, transcendentals=0),
    )(
        layer_input.reshape(2, 64, 1024),
        attn_out.reshape(4, 4, 128, 128),
        out_grad,
        q_grad.reshape(4, 8, 64, 128),
        k_grad.reshape(4, 8, 64, 128),
        q_weight,
        k_weight[0],
        o_weight,
    )
    return (
        ig.reshape(128, 1024),
        ag.reshape(2048, 128),
        qwg,
        kwg[None],
        owg,
    )


def solution(mesh):
    return jax.shard_map(
        shards,
        mesh=mesh,
        in_specs=(
            P("seq", ("row", "col")),
            P(("row", "col"), "seq"),
            P("seq", ("row", "col")),
            P(("row", "col"), "seq"),
            P(("row", "col"), "seq"),
            P(("row", "col"), "seq"),
            P("seq", ("row", "col"), None),
            P("seq", ("row", "col")),
        ),
        out_specs=(
            P("seq", ("row", "col")),
            P(("row", "col"), "seq"),
            P(("row", "col"), "seq"),
            P("seq", ("row", "col"), None),
            P("seq", ("row", "col")),
        ),
        check_vma=False,
    )
```

time: 213 us -> 229 us (1.075)
  Pallas kernels: 207 us -> 223 us
    pallas_call x1, Pallas kernels: 207 us -> 223 us  [shards(): pl.pallas_call(kernel, out_shape=[jax.ShapeDtypeStruct(*shape) for shape...]
where the time goes in v2:
time: 229 us; the launch traced here: 228 us
  Pallas kernels  223 us (97%)
  local copies, waits for them, and re-layouts  5.25 us (2%)
    pallas_call x1, Pallas kernels, shards(): pl.pallas_call(kernel, out_shape=[jax.ShapeDtypeStruct(*shape) for shape...  223 us
    unnamed x13, local copies, waits for them, and re-layouts  5.25 us

profile of v2, /device:TPU:2, one launch (start us, length us, event | category | flops | bytes accessed | tf_op | source)
XLA Modules:
  0.0 228.5 jit_solution(8415193346996328053)
XLA Ops:
  0.6 222.6 %shard_map.119 = (bf16[2,64,1024]{2,1,0:T(8,128)(2,1)}, bf16[4,4,128,128]{3,2,1,0:T(8,128)(2,1)}, f32[1024,128]{1,0:T(8,128)}, f32[128,128]{1,0:T(8,128)}, f32[128,1024]{1,0:T(8,128)}) custom-call(bf16[2,64,1024]{2,1,0:T(8,128)(2,1)} %bitcast.14, bf16[4,4,128,128]{3,2,1,0:T(8,128)(2,1)} %bitcast.11, bf16[128,1024]{1,0:T(8,128)(2,1)} %og.1, ...), custom_call_target="tpu_custom_call" | custom-call | flops 14000000000 | bytes 5000000 | tf_op jit(solution)/shard_map/pallas_call | solution.py:474
  223.2 0.0 copy-start.2
  223.2 1.7 copy.18
  224.9 0.0 copy-done.2
  225.0 0.0 copy-start.1
  225.0 0.8 copy.19
  225.7 0.4 copy-done.1
  226.2 0.0 copy-start.3
  226.2 0.0 copy-start
  226.2 0.8 copy.20
  227.0 0.1 copy-done.3
  227.0 0.6 copy.21
  227.7 0.0 copy-done
  227.7 0.8 copy.22
Async XLA Ops:
  223.2 1.7 copy-start.2
  225.0 1.2 copy-start.1
  226.2 0.9 copy-start.3
  226.2 1.5 copy-start

commit v3 on v2

--- a/solution.py
+++ b/solution.py
@@ -253,48 +253,82 @@
     def og_slot(zz, half):
         return ogt.at[lax.div(zz, 2), part_of(128, half), at1024(lax.rem(zz, 2))]
 
-    li_slot = lit.at[x, y, :, at1024(zlo)]
-    li_own = place(li.at[zlo], li_slot)
-    li_sent = send(li.at[1 - zlo], li_slot, zpartner)
+    og_own = place(og, og_slot(z, None))
     for r in range(2):
         post(
             ow.at[pl.ds(r * 64, 64)], owt.at[x, yhi * 2 + r, :, at1024(zlo)], spread_ow[r], zlo
         )
+    og_own.wait()
+    og_step, og_done = ring_gather(z_ring, og_slot)
+    for j in range(4):
+        post(ao.at[j], aot.at[yhi, :, :, at128(x)], spread_ao[j], 2 + x)
+    li_slot = lit.at[x, y, :, at1024(zlo)]
+    li_own = place(li.at[zlo], li_slot)
+    li_sent = send(li.at[1 - zlo], li_slot, zpartner)
     km_own = place(kw, km.at[zlo, ylo, zh])
     km_sent = send(kw, km.at[zlo, ylo, zh], ypartner)
     qw_own = place(qw, qw_slot(z, None))
-    og_own = place(og, og_slot(z, None))
-    q_own, q_copies = spread(q, qkt.at[quarter, :, :, at128(zh)])
-    qw_own.wait()
-    qw_step, qw_done = ring_gather(z_ring, qw_slot)
-    k_own, k_copies = spread(k, kbuf.at[zh, zlo])
+    for b in range(2):
+        collect(owt.at[x, y, :, pl.ds(b * 1024, 1024)], b)
+    ow_all = Gather(owt)
+    og_step(2)
+    ow_all.inner()
     li_own.wait()
     li_sent.wait_recv()
     li_all = Gather(lit)
-    for b in range(2):
-        collect(owt.at[x, y, :, pl.ds(b * 1024, 1024)], b)
-    ow_all = Gather(owt)
-    for j in range(4):
-        post(ao.at[j], aot.at[yhi, :, :, at128(x)], spread_ao[j], 2 + x)
+    og_step(3)
+    q_own, q_copies = spread(q, qkt.at[quarter, :, :, at128(zh)])
+    li_all.inner()
+    og_step(4)
+    k_own, k_copies = spread(k, kbuf.at[zh, zlo])
+    qw_own.wait()
+    qw_step, qw_done = ring_gather(z_ring, qw_slot)
+    ow_all.outer()
+
+    for i in range(4):
+        collect(aot.at[col, :, :, pl.ds(i * 128, 128)], 2 + i)
+    ao_shared = send(aot.at[col], aot.at[col], sibling)
+    og_done()
+    ao_shared.wait_recv()
+    for h in range(2):
+        def block(i, _, h=h):
+            cols = pl.ds(pl.multiple_of(i * 512, 512), 512)
+            part = lax.dot_general(
+                aot[h].reshape(512, 512), ogt[:, :, cols].reshape(512, 512),
+                (((0,), (0,)), ((), ())), preferred_element_type=F32,
+            )
+            owg[:, pl.ds(2 * h, 2), :, cols] = part.reshape(4, 2, 64, 512)
+            return 0
+        lax.fori_loop(0, 4, block, 0)
+    owg_sum = Reduce(owg, owg_got)
     km_own.wait()
     km_sent.wait_recv()
     km_step, km_done = ring_gather(z_ring, km_slot)
+    qw_step(2)
+    ow_all.inner()
+    li_all.outer()
+
+    ow_all.done()
+    for h in range(2):
+        part = lax.dot_general(
+            ogt[...].reshape(512, 2048), owt[:, pl.ds(2 * h, 2)].reshape(512, 2048),
+            (((1,), (1,)), ((), ())), preferred_element_type=F32,
+        ).reshape(4, 2, 64, 512)
+        ig[h, :, :, pl.ds(0, 512)] = part[:, 0]
+        ig[h, :, :, pl.ds(512, 512)] = part[:, 1]
+    ag_sent = send(ig.at[1 - col, :, :, pl.ds(0, 1024)], agr, sibling)
+    qw_step(3)
+    km_step(2)
+    ag_sent.wait()
+    for half in range(2):
+        cols = pl.ds(half * 512, 512)
+        agb[:, pl.ds(half * 64, 64), :] = (ig[col, :, :, cols] + agr[:, :, cols]).astype(BF16)
+    owg_sum.second()
+    for i in range(4):
+        post(agb.at[:, :, pl.ds(i * 128, 128)], ag_out.at[y], return_ag[i], 6 + y)
     li_all.inner()
-    ow_all.inner()
-    qw_step(2)
-    og_own.wait()
-    og_step, og_done = ring_gather(z_ring, og_slot)
-    km_step(2)
-    li_all.outer()
-    qw_step(3)
+    qw_step(4)
     km_step(3)
-    ow_all.outer()
-    og_step(2)
-    qw_step(4)
-    km_step(4)
-    li_all.inner()
-    og_step(3)
-    ow_all.inner()
 
     k_own.wait()
     arrive(k_copies)
@@ -308,29 +342,10 @@
     q_own.wait()
     arrive(q_copies)
     q_shared = [send(v, v, sibling) for v in [qkt.at[lo * 2 + col] for lo in range(2)]]
-
-    qw_done()
-    km_done()
-    for lo in range(2):
-        keys = km[lo].reshape(1024, 128)
-        w3[lo, :, pl.ds(512, 128)] = keys
-        w3[lo, :, pl.ds(640, 128)] = keys
+    km_step(4)
+    li_all.done()
     arrive(q_shared)
-    for lo in range(2):
-        def block(i, _, lo=lo):
-            cols = pl.ds(pl.multiple_of(lo * 1024 + i * 256, 256), 256)
-            rows = pl.ds(pl.multiple_of(i * 256, 256), 256)
-            part = lax.dot_general(
-                qkt[...].reshape(1024, 768), w3[lo, rows, :],
-                (((1,), (1,)), ((), ())), preferred_element_type=F32,
-            )
-            ig[:, :, :, cols] = part.reshape(4, 4, 64, 256)
-            return 0
-        lax.fori_loop(0, 4, block, 0)
-    ig_sum = Reduce(ig, ig_got)
-    og_step(4)
-
-    li_all.done()
+
     for lo in range(2):
         def block(i, _, lo=lo):
             cols = pl.ds(pl.multiple_of(lo * 1024 + i * 256, 256), 256)
@@ -354,67 +369,52 @@
         lambda d: kw_far.at[d], lambda d, s: kw_full.at[d, s],
     )
 
-    for i in range(4):
-        collect(aot.at[col, :, :, pl.ds(i * 128, 128)], 2 + i)
-    ao_shared = send(aot.at[col], aot.at[col], sibling)
-    ow_all.done()
-    og_done()
-    for h in range(2):
-        part = lax.dot_general(
-            ogt[...].reshape(512, 2048), owt[:, pl.ds(2 * h, 2)].reshape(512, 2048),
-            (((1,), (1,)), ((), ())), preferred_element_type=F32,
-        ).reshape(4, 2, 64, 512)
-        owg[h, :, :, pl.ds(0, 512)] = part[:, 0]
-        owg[h, :, :, pl.ds(512, 512)] = part[:, 1]
-    ag_sent = send(owg.at[1 - col, :, :, pl.ds(0, 1024)], agr, sibling)
+    qw_done()
+    km_done()
+    for lo in range(2):
+        keys = km[lo].reshape(1024, 128)
+        w3[lo, :, pl.ds(512, 128)] = keys
+        w3[lo, :, pl.ds(640, 128)] = keys
+    for lo in range(2):
+        def block(i, _, lo=lo):
+            cols = pl.ds(pl.multiple_of(lo * 1024 + i * 256, 256), 256)
+            rows = pl.ds(pl.multiple_of(i * 256, 256), 256)
+            part = lax.dot_general(
+                qkt[...].reshape(1024, 768), w3[lo, rows, :],
+                (((1,), (1,)), ((), ())), preferred_element_type=F32,
+            )
+            ig[:, :, :, cols] = part.reshape(4, 4, 64, 256)
+            return 0
+        lax.fori_loop(0, 4, block, 0)
+    ig_sum = Reduce(ig, ig_got)
+
     qwg_step(2)
     kwg_step(2)
-    ag_sent.wait()
-    for half in range(2):
-        cols = pl.ds(half * 512, 512)
-        agb[:, pl.ds(half * 64, 64), :] = (owg[col, :, :, cols] + agr[:, :, cols]).astype(BF16)
-
-    ao_shared.wait_recv()
-    for h in range(2):
-        def block(i, _, h=h):
-            cols = pl.ds(pl.multiple_of(i * 512, 512), 512)
-            part = lax.dot_general(
-                aot[h].reshape(512, 512), ogt[:, :, cols].reshape(512, 512),
-                (((0,), (0,)), ((), ())), preferred_element_type=F32,
-            )
-            owg[:, pl.ds(2 * h, 2), :, cols] = part.reshape(4, 2, 64, 512)
-            return 0
-        lax.fori_loop(0, 4, block, 0)
-    owg_sum = Reduce(owg, owg_got)
-    for i in range(4):
-        post(agb.at[:, :, pl.ds(i * 128, 128)], ag_out.at[y], return_ag[i], 6 + y)
-
-    ig_sum.second()
+    owg_sum.inner()
     qwg_step(3)
     kwg_step(3)
     owg_sum.second()
+    ig_sum.second()
     qwg_step(4)
     kwg_step(4)
-    ig_sum.inner()
-    ig_sum.second()
-    kwg_mine = kwg_total()
-    kwg_sent = send(kwg_mine.at[1 - ylo], kwy, ypartner)
-    qwg_own = place(qwg_total(), qwg_out)
-    owg_sum.inner()
-    ig_sum.total()
-    fin[...] = ig[x, y].astype(BF16)
-    ig_own = place(fin.at[:, at1024(zlo)], ig_out.at[zlo])
-    ig_sent = send(fin.at[:, at1024(1 - zlo)], ig_out.at[zlo], zpartner)
-    kwg_sent.wait_recv()
-    kwy[...] = kwy[...] + kwg_mine[ylo]
-    kwg_own = place(kwy, kwg_out)
-    owg_sum.second()
     owg_sum.total()
     for b in range(2):
         post(
             owg.at[x, y, :, pl.ds(b * 1024, 1024)],
             owg_out.at[pl.ds(pl.multiple_of(ylo * 64, 64), 64)], return_ow[b], 10 + ylo,
         )
+    kwg_mine = kwg_total()
+    kwg_sent = send(kwg_mine.at[1 - ylo], kwy, ypartner)
+    qwg_own = place(qwg_total(), qwg_out)
+    ig_sum.inner()
+    kwg_sent.wait_recv()
+    kwy[...] = kwy[...] + kwg_mine[ylo]
+    kwg_own = place(kwy, kwg_out)
+    ig_sum.second()
+    ig_sum.total()
+    fin[...] = ig[x, y].astype(BF16)
+    ig_own = place(fin.at[:, at1024(zlo)], ig_out.at[zlo])
+    ig_sent = send(fin.at[:, at1024(1 - zlo)], ig_out.at[zlo], zpartner)
     for copy in sent:
         if copy is not ag_sent:
             copy.wait_send()
@@ -428,6 +428,18 @@
         collect(owg_out.at[pl.ds(r * 64, 64)], 10 + r)
     ig_sent.wait_recv()
     for copy in (qwg_own, ig_own, kwg_own):
+        copy.wait()
+
+
+def finish(*refs):
+    sems = refs[-1]
+    count = (len(refs) - 1) // 2
+    copies = [
+        pltpu.make_async_copy(refs[n], refs[count + n], sems.at[n]) for n in range(count)
+    ]
+    for copy in copies:
+        copy.start()
+    for copy in copies:
         copy.wait()
 
 
@@ -491,13 +503,16 @@
         k_weight[0],
         o_weight,
     )
-    return (
-        ig.reshape(128, 1024),
-        ag.reshape(2048, 128),
-        qwg,
-        kwg[None],
-        owg,
-    )
+    parts = (ig.reshape(128, 1024), ag.reshape(2048, 128), qwg, kwg, owg)
+    ig, ag, qwg, kwg, owg = pl.pallas_call(
+        finish,
+        out_shape=[jax.ShapeDtypeStruct(part.shape, part.dtype) for part in parts],
+        in_specs=[pl.BlockSpec(memory_space=pl.ANY)] * 5,
+        out_specs=[pl.BlockSpec(memory_space=pl.ANY)] * 5,
+        scratch_shapes=[pltpu.SemaphoreType.DMA((5,))],
+        compiler_params=pltpu.CompilerParams(vmem_limit_bytes=63 * 2**20),
+    )(*parts)
+    return ig, ag, qwg, kwg[None], owg
 
 
 def solution(mesh):

time: 229 us -> 286 us (1.25)
  Pallas kernels: 223 us -> 284 us
  local copies, waits for them, and re-layouts: 5.25 us -> 0 us
    pallas_call x0 -> x1, Pallas kernels: none -> 58.7 us  [shards(): pl.pallas_call(finish, out_shape=[jax.ShapeDtypeStruct(part.shape, part.d...]
    unnamed x13 -> x0, local copies, waits for them, and re-layouts: 5.25 us -> none
where the time goes in v3:
time: 286 us; the launch traced here: 285 us
  Pallas kernels  284 us (99%)
    pallas_call x1, Pallas kernels, shards(): pl.pallas_call(kernel, out_shape=[jax.ShapeDtypeStruct(*shape) for shape...  225 us
    pallas_call x1, Pallas kernels, shards(): pl.pallas_call(finish, out_shape=[jax.ShapeDtypeStruct(part.shape, part.d...  58.7 us

profile of v3, /device:TPU:2, one launch (start us, length us, event | category | flops | bytes accessed | tf_op | source)
XLA Modules:
  0.0 284.7 jit_solution(5648192946217343688)
XLA Ops:
  0.6 225.4 %shard_map.119 = (bf16[2,64,1024]{2,1,0:T(8,128)(2,1)}, bf16[4,4,128,128]{3,2,1,0:T(8,128)(2,1)}, f32[1024,128]{1,0:T(8,128)}, f32[128,128]{1,0:T(8,128)}, f32[128,1024]{1,0:T(8,128)}) custom-call(bf16[2,64,1024]{2,1,0:T(8,128)(2,1)} %bitcast.13, bf16[4,4,128,128]{3,2,1,0:T(8,128)(2,1)} %bitcast.10, bf16[128,1024]{1,0:T(8,128)(2,1)} %og.1, ...), custom_call_target="tpu_custom_call" | custom-call | flops 14000000000 | bytes 5000000 | tf_op jit(solution)/shard_map/pallas_call | solution.py:486
  226.0 58.7 %shard_map.120 = (bf16[128,1024]{1,0:T(8,128)(2,1)}, bf16[2048,128]{1,0:T(8,128)(2,1)}, f32[1024,128]{1,0:T(8,128)}, f32[128,128]{1,0:T(8,128)}, f32[128,1024]{1,0:T(8,128)}) custom-call(bf16[128,1024]{1,0:T(8,128)(2,1)} %bitcast.9, bf16[2048,128]{1,0:T(8,128)(2,1)} %bitcast.8, f32[1024,128]{1,0:T(8,128)} %get-tuple-element.17.refs_2_, ...), custom_call_target="tpu_custom_call" | custom-call | tf_op jit(solution)/shard_map/pallas_call | solution.py:507

commit v4 on v3

--- a/solution.py
+++ b/solution.py
@@ -253,41 +253,47 @@
     def og_slot(zz, half):
         return ogt.at[lax.div(zz, 2), part_of(128, half), at1024(lax.rem(zz, 2))]
 
-    og_own = place(og, og_slot(z, None))
+    for j in range(4):
+        post(ao.at[j], aot.at[yhi, :, :, at128(x)], spread_ao[j], 2 + x)
     for r in range(2):
         post(
             ow.at[pl.ds(r * 64, 64)], owt.at[x, yhi * 2 + r, :, at1024(zlo)], spread_ow[r], zlo
         )
-    og_own.wait()
-    og_step, og_done = ring_gather(z_ring, og_slot)
-    for j in range(4):
-        post(ao.at[j], aot.at[yhi, :, :, at128(x)], spread_ao[j], 2 + x)
+    og_own = place(og, og_slot(z, None))
     li_slot = lit.at[x, y, :, at1024(zlo)]
     li_own = place(li.at[zlo], li_slot)
     li_sent = send(li.at[1 - zlo], li_slot, zpartner)
-    km_own = place(kw, km.at[zlo, ylo, zh])
-    km_sent = send(kw, km.at[zlo, ylo, zh], ypartner)
-    qw_own = place(qw, qw_slot(z, None))
     for b in range(2):
         collect(owt.at[x, y, :, pl.ds(b * 1024, 1024)], b)
     ow_all = Gather(owt)
-    og_step(2)
-    ow_all.inner()
+    og_own.wait()
+    og_step, og_done = ring_gather(z_ring, og_slot)
     li_own.wait()
     li_sent.wait_recv()
     li_all = Gather(lit)
-    og_step(3)
+    ow_all.inner()
     q_own, q_copies = spread(q, qkt.at[quarter, :, :, at128(zh)])
     li_all.inner()
-    og_step(4)
-    k_own, k_copies = spread(k, kbuf.at[zh, zlo])
-    qw_own.wait()
-    qw_step, qw_done = ring_gather(z_ring, qw_slot)
+    og_step(2)
+    km_own = place(kw, km.at[zlo, ylo, zh])
+    km_sent = send(kw, km.at[zlo, ylo, zh], ypartner)
     ow_all.outer()
-
     for i in range(4):
         collect(aot.at[col, :, :, pl.ds(i * 128, 128)], 2 + i)
     ao_shared = send(aot.at[col], aot.at[col], sibling)
+    km_own.wait()
+    km_sent.wait_recv()
+    km_step, km_done = ring_gather(z_ring, km_slot)
+    li_all.outer()
+    og_step(3)
+    qw_own = place(qw, qw_slot(z, None))
+    ow_all.inner()
+    km_step(2)
+    og_step(4)
+    km_step(3)
+    qw_own.wait()
+    qw_step, qw_done = ring_gather(z_ring, qw_slot)
+    li_all.inner()
     og_done()
     ao_shared.wait_recv()
     for h in range(2):
@@ -301,13 +307,7 @@
             return 0
         lax.fori_loop(0, 4, block, 0)
     owg_sum = Reduce(owg, owg_got)
-    km_own.wait()
-    km_sent.wait_recv()
-    km_step, km_done = ring_gather(z_ring, km_slot)
-    qw_step(2)
-    ow_all.inner()
-    li_all.outer()
-
+    k_own, k_copies = spread(k, kbuf.at[zh, zlo])
     ow_all.done()
     for h in range(2):
         part = lax.dot_general(
@@ -317,19 +317,15 @@
         ig[h, :, :, pl.ds(0, 512)] = part[:, 0]
         ig[h, :, :, pl.ds(512, 512)] = part[:, 1]
     ag_sent = send(ig.at[1 - col, :, :, pl.ds(0, 1024)], agr, sibling)
-    qw_step(3)
-    km_step(2)
+    qw_step(2)
     ag_sent.wait()
     for half in range(2):
         cols = pl.ds(half * 512, 512)
         agb[:, pl.ds(half * 64, 64), :] = (ig[col, :, :, cols] + agr[:, :, cols]).astype(BF16)
-    owg_sum.second()
     for i in range(4):
         post(agb.at[:, :, pl.ds(i * 128, 128)], ag_out.at[y], return_ag[i], 6 + y)
-    li_all.inner()
-    qw_step(4)
-    km_step(3)
-
+    owg_sum.second()
+    km_step(4)
     k_own.wait()
     arrive(k_copies)
     for lo in range(2):
@@ -339,10 +335,11 @@
         high = total.astype(BF16)
         qkt[lo * 2 + col, :, :, pl.ds(512, 128)] = high
         qkt[lo * 2 + col, :, :, pl.ds(640, 128)] = (total - high.astype(F32)).astype(BF16)
+    qw_step(3)
     q_own.wait()
     arrive(q_copies)
     q_shared = [send(v, v, sibling) for v in [qkt.at[lo * 2 + col] for lo in range(2)]]
-    km_step(4)
+    qw_step(4)
     li_all.done()
     arrive(q_shared)
 
@@ -389,28 +386,28 @@
     ig_sum = Reduce(ig, ig_got)
 
     qwg_step(2)
+    ig_sum.second()
     kwg_step(2)
+    kwg_step(3)
+    qwg_step(3)
+    kwg_step(4)
+    qwg_step(4)
+    kwg_mine = kwg_total()
+    kwg_sent = send(kwg_mine.at[1 - ylo], kwy, ypartner)
     owg_sum.inner()
-    qwg_step(3)
-    kwg_step(3)
+    ig_sum.inner()
+    kwg_sent.wait_recv()
+    kwy[...] = kwy[...] + kwg_mine[ylo]
+    kwg_own = place(kwy, kwg_out)
     owg_sum.second()
     ig_sum.second()
-    qwg_step(4)
-    kwg_step(4)
+    qwg_own = place(qwg_total(), qwg_out)
     owg_sum.total()
     for b in range(2):
         post(
             owg.at[x, y, :, pl.ds(b * 1024, 1024)],
             owg_out.at[pl.ds(pl.multiple_of(ylo * 64, 64), 64)], return_ow[b], 10 + ylo,
         )
-    kwg_mine = kwg_total()
-    kwg_sent = send(kwg_mine.at[1 - ylo], kwy, ypartner)
-    qwg_own = place(qwg_total(), qwg_out)
-    ig_sum.inner()
-    kwg_sent.wait_recv()
-    kwy[...] = kwy[...] + kwg_mine[ylo]
-    kwg_own = place(kwy, kwg_out)
-    ig_sum.second()
     ig_sum.total()
     fin[...] = ig[x, y].astype(BF16)
     ig_own = place(fin.at[:, at1024(zlo)], ig_out.at[zlo])
@@ -432,15 +429,8 @@
 
 
 def finish(*refs):
-    sems = refs[-1]
-    count = (len(refs) - 1) // 2
-    copies = [
-        pltpu.make_async_copy(refs[n], refs[count + n], sems.at[n]) for n in range(count)
-    ]
-    for copy in copies:
-        copy.start()
-    for copy in copies:
-        copy.wait()
+    for source, target in zip(refs[:5], refs[5:]):
+        target[...] = source[...]
 
 
 def shards(layer_input, attn_out, out_grad, q_grad, k_grad, q_weight, k_weight, o_weight):
@@ -507,10 +497,8 @@
     ig, ag, qwg, kwg, owg = pl.pallas_call(
         finish,
         out_shape=[jax.ShapeDtypeStruct(part.shape, part.dtype) for part in parts],
-        in_specs=[pl.BlockSpec(memory_space=pl.ANY)] * 5,
-        out_specs=[pl.BlockSpec(memory_space=pl.ANY)] * 5,
-        scratch_shapes=[pltpu.SemaphoreType.DMA((5,))],
-        compiler_params=pltpu.CompilerParams(vmem_limit_bytes=63 * 2**20),
+        in_specs=[pl.BlockSpec(memory_space=pltpu.VMEM)] * 5,
+        out_specs=[pl.BlockSpec(memory_space=pltpu.VMEM)] * 5,
     )(*parts)
     return ig, ag, qwg, kwg[None], owg
 

time: 286 us -> 191 us (0.67)
  Pallas kernels: 284 us -> 189 us
    pallas_call x1, Pallas kernels: 58.7 us -> 2.74 us  [shards(): pl.pallas_call(finish, out_shape=[jax.ShapeDtypeStruct(part.shape, part.d...]
    pallas_call x1, Pallas kernels: 225 us -> 187 us  [shards(): pl.pallas_call(kernel, out_shape=[jax.ShapeDtypeStruct(*shape) for shape...]
where the time goes in v4:
time: 191 us; the launch traced here: 190 us
  Pallas kernels  189 us (99%)
    pallas_call x1, Pallas kernels, shards(): pl.pallas_call(kernel, out_shape=[jax.ShapeDtypeStruct(*shape) for shape...  187 us

profile of v4, /device:TPU:2, one launch (start us, length us, event | category | flops | bytes accessed | tf_op | source)
XLA Modules:
  0.0 190.0 jit_solution(5756968901666194325)
XLA Ops:
  0.6 186.6 %shard_map.119 = (bf16[2,64,1024]{2,1,0:T(8,128)(2,1)}, bf16[4,4,128,128]{3,2,1,0:T(8,128)(2,1)}, f32[1024,128]{1,0:T(8,128)}, f32[128,128]{1,0:T(8,128)}, f32[128,1024]{1,0:T(8,128)}) custom-call(bf16[2,64,1024]{2,1,0:T(8,128)(2,1)} %bitcast.13, bf16[4,4,128,128]{3,2,1,0:T(8,128)(2,1)} %bitcast.10, bf16[128,1024]{1,0:T(8,128)(2,1)} %og.1, ...), custom_call_target="tpu_custom_call" | custom-call | flops 14000000000 | bytes 5000000 | tf_op jit(solution)/shard_map/pallas_call | solution.py:476
  187.3 2.7 %shard_map.120 = (bf16[128,1024]{1,0:T(8,128)(2,1)}, bf16[2048,128]{1,0:T(8,128)(2,1)}, f32[1024,128]{1,0:T(8,128)}, f32[128,128]{1,0:T(8,128)}, f32[128,1024]{1,0:T(8,128)}) custom-call(bf16[128,1024]{1,0:T(8,128)(2,1)} %bitcast.9, bf16[2048,128]{1,0:T(8,128)(2,1)} %bitcast.8, f32[1024,128]{1,0:T(8,128)} %get-tuple-element.17.refs_2_, ...), custom_call_target="tpu_custom_call" | custom-call | tf_op jit(solution)/shard_map/pallas_call | solution.py:497

commit v5 on v4

--- a/solution.py
+++ b/solution.py
@@ -6,7 +6,7 @@
 from jax.sharding import PartitionSpec as P
 
 MESH = pl.DeviceIdType.MESH
-COPIES = 160
+COPIES = 176
 F32 = jnp.float32
 BF16 = jnp.bfloat16
 
@@ -27,10 +27,10 @@
     li, ao, og, q, k, qw, kw, ow,
     ig_out, ag_out, qwg_out, kwg_out, owg_out,
     lit, owt, ogt, qkt, aot, w3, km, kbuf,
-    ig, owg, ig_got, owg_got,
+    ig, owg, ig_got, ow_far, ow_full, owy,
     qwg, kwg, qw_far, qw_full, kw_far, kw_full, kwy,
-    agr, agb, fin,
-    ssem, rsem, lsem, gsem,
+    ag, agr, agb, fin,
+    ssem, rsem, lsem,
 ):
     seq = lax.axis_index("seq")
     x, y, zh = lax.div(seq, 16), lax.rem(lax.div(seq, 4), 4), lax.rem(seq, 4)
@@ -39,9 +39,6 @@
     yhi, ylo = lax.div(y, 2), lax.rem(y, 2)
     quarter = zlo * 2 + col
 
-    def at(xx, yy, lo, core):
-        return (xx * 16 + yy * 4 + zh, lo, core)
-
     def device(dx, dy, dz):
         zz = rem(z + dz, 8)
         return (
@@ -49,35 +46,27 @@
         )
 
     zs = [device(0, 0, d) for d in range(1, 8)]
-    sibling = at(x, y, zlo, 1 - col)
+    sibling = (seq, zlo, 1 - col)
     zpartner = device(0, 0, 1 - 2 * zlo)
     ypartner = device(0, 1 - 2 * ylo, 0)
     x_ring = (4, x, device(-1, 0, 0), device(1, 0, 0))
     y_ring = (4, y, device(0, -1, 0), device(0, 1, 0))
     z_ring = (8, z, device(0, 0, -1), device(0, 0, 1))
 
-    square = ylo == zlo
-    home = jnp.logical_and(x == quarter, y == col * 2 + zlo)
-    spread_ow = [(at(x, yhi * 2 + r, ylo, col), jnp.logical_and(square, ylo == r)) for r in range(2)]
-    return_ow = [(at(x, yhi * 2 + zlo, b, col), jnp.logical_and(square, zlo == b)) for b in range(2)]
-    spread_ao = [(at(quarter, j, ylo, yhi), jnp.logical_and(home, y == j)) for j in range(4)]
-    return_ag = [
-        (at(i, col * 2 + zlo, lax.div(x, 2), lax.rem(x, 2)), jnp.logical_and(home, x == i))
-        for i in range(4)
+    zh_ring = (4, zh, device(0, 0, -2), device(0, 0, 2))
+
+    places = [
+        (rem(y + d, 4), lo, device(0, d, dz)) for d in range(4)
+        for lo, dz in ((zlo, 0), (1 - zlo, 1 - 2 * zlo))
     ]
 
     barrier = pltpu.get_barrier_semaphore()
-    peers = list(x_ring[2:]) + list(y_ring[2:]) + zs + [sibling]
+    peers = list(x_ring[2:]) + [place[2] for place in places[1:]] + zs + [sibling]
     for peer in peers:
         pl.semaphore_signal(barrier, inc=1, device_id=peer, device_id_type=MESH)
-    for peer, own in spread_ow + return_ow + spread_ao + return_ag:
-        @pl.when(jnp.logical_not(own))
-        def _(peer=peer):
-            pl.semaphore_signal(barrier, inc=1, device_id=peer, device_id_type=MESH)
-    count = len(peers) + 12 - 2 * square.astype(jnp.int32) - 2 * home.astype(jnp.int32)
-    pl.semaphore_wait(barrier, count)
-
-    sent, local, guarded = [], [], []
+    pl.semaphore_wait(barrier, len(peers))
+
+    sent, local, last, stored = [], [], [], []
 
     def send(src, dst, to):
         n = len(sent)
@@ -94,26 +83,6 @@
         copy.start()
         local.append(copy)
         return copy
-
-    def post(src, dst, partner, slot):
-        to, own = partner
-        copy = pltpu.make_async_remote_copy(
-            src_ref=src, dst_ref=dst, send_sem=gsem.at[16 + len(guarded)],
-            recv_sem=gsem.at[slot], device_id=to, device_id_type=MESH,
-        )
-
-        @pl.when(jnp.logical_not(own))
-        def _():
-            copy.start()
-
-        @pl.when(own)
-        def _():
-            pltpu.make_async_copy(src, dst, gsem.at[slot]).start()
-
-        guarded.append((copy, own))
-
-    def collect(dst, slot):
-        pltpu.make_async_copy(dst, dst, gsem.at[slot]).wait()
 
     def arrive(copies):
         for copy in copies:
@@ -250,82 +219,87 @@
     def km_slot(zz, half):
         return km.at[lax.rem(zz, 2), part_of(2, half), lax.div(zz, 2)]
 
-    def og_slot(zz, half):
-        return ogt.at[lax.div(zz, 2), part_of(128, half), at1024(lax.rem(zz, 2))]
-
-    for j in range(4):
-        post(ao.at[j], aot.at[yhi, :, :, at128(x)], spread_ao[j], 2 + x)
-    for r in range(2):
-        post(
-            ow.at[pl.ds(r * 64, 64)], owt.at[x, yhi * 2 + r, :, at1024(zlo)], spread_ow[r], zlo
-        )
-    og_own = place(og, og_slot(z, None))
+    og_slot = ogt.at[x, zh, :, at1024(zlo)]
+    og_own = place(og.at[zlo], og_slot)
+    og_sent = send(og.at[1 - zlo], og_slot, zpartner)
+    km_own = place(kw, km.at[zlo, ylo, zh])
+    km_sent = send(kw, km.at[zlo, ylo, zh], ypartner)
+    qw_own = place(qw, qw_slot(z, None))
     li_slot = lit.at[x, y, :, at1024(zlo)]
     li_own = place(li.at[zlo], li_slot)
     li_sent = send(li.at[1 - zlo], li_slot, zpartner)
-    for b in range(2):
-        collect(owt.at[x, y, :, pl.ds(b * 1024, 1024)], b)
-    ow_all = Gather(owt)
     og_own.wait()
-    og_step, og_done = ring_gather(z_ring, og_slot)
+    og_sent.wait_recv()
+    og_step, og_done = ring_gather(zh_ring, lambda i, h: ogt.at[x, i, part_of(64, h)])
     li_own.wait()
     li_sent.wait_recv()
     li_all = Gather(lit)
-    ow_all.inner()
-    q_own, q_copies = spread(q, qkt.at[quarter, :, :, at128(zh)])
     li_all.inner()
+    li_all.outer()
     og_step(2)
-    km_own = place(kw, km.at[zlo, ylo, zh])
-    km_sent = send(kw, km.at[zlo, ylo, zh], ypartner)
-    ow_all.outer()
-    for i in range(4):
-        collect(aot.at[col, :, :, pl.ds(i * 128, 128)], 2 + i)
-    ao_shared = send(aot.at[col], aot.at[col], sibling)
+    og_done()
+    og_step, og_done = ring_gather(x_ring, lambda i, h: ogt.at[i, part_of(4, h)])
+    ao_slot = aot.at[quarter, :, :, at128(y)]
+    ao_own = place(ao.at[y, :, zlo], ao_slot)
+    ao_copies = [send(ao.at[j, :, lo], ao_slot, to) for j, lo, to in places[1:]]
     km_own.wait()
     km_sent.wait_recv()
     km_step, km_done = ring_gather(z_ring, km_slot)
-    li_all.outer()
-    og_step(3)
-    qw_own = place(qw, qw_slot(z, None))
-    ow_all.inner()
-    km_step(2)
-    og_step(4)
-    km_step(3)
+    ow_slot = owt.at[y, :, at1024(zlo)]
+    ow_own = place(ow, ow_slot)
+    ow_sent = send(ow, ow_slot, zpartner)
+    ao_own.wait()
+    arrive(ao_copies)
+    ao_shared = [send(v, v, sibling) for v in [aot.at[lo * 2 + col] for lo in range(2)]]
+    k_own, k_copies = spread(k, kbuf.at[zh, zlo])
+    ow_own.wait()
+    ow_sent.wait_recv()
+    ow_step, ow_done = ring_gather(y_ring, lambda j, h: owt.at[j, part_of(128, h)])
+    og_step(2)
     qw_own.wait()
     qw_step, qw_done = ring_gather(z_ring, qw_slot)
+    ow_step(2)
+    q_own, q_copies = spread(q, qkt.at[quarter, :, :, at128(zh)])
+    km_step(2)
     li_all.inner()
     og_done()
-    ao_shared.wait_recv()
-    for h in range(2):
-        def block(i, _, h=h):
-            cols = pl.ds(pl.multiple_of(i * 512, 512), 512)
+    arrive(ao_shared)
+    for lo in range(2):
+        for i in range(1):
             part = lax.dot_general(
-                aot[h].reshape(512, 512), ogt[:, :, cols].reshape(512, 512),
+                aot[...].reshape(1024, 512),
+                ogt[:, :, :, pl.ds(lo * 1024 + 0 + i * 512, 512)].reshape(1024, 512),
                 (((0,), (0,)), ((), ())), preferred_element_type=F32,
             )
-            owg[:, pl.ds(2 * h, 2), :, cols] = part.reshape(4, 2, 64, 512)
-            return 0
-        lax.fori_loop(0, 4, block, 0)
-    owg_sum = Reduce(owg, owg_got)
-    k_own, k_copies = spread(k, kbuf.at[zh, zlo])
-    ow_all.done()
-    for h in range(2):
-        part = lax.dot_general(
-            ogt[...].reshape(512, 2048), owt[:, pl.ds(2 * h, 2)].reshape(512, 2048),
+            owg[0, :, lo, :, pl.ds(i * 512, 512)] = part.reshape(4, 128, 512)
+    owg_a_step, owg_a_total = ring_reduce(
+        y_ring, lambda j: owg.at[0, j], lambda d: ow_far.at[0, d],
+        lambda d, s: ow_full.at[0, d, s],
+    )
+    qw_step(2)
+    for lo in range(2):
+        for i in range(1):
+            part = lax.dot_general(
+                aot[...].reshape(1024, 512),
+                ogt[:, :, :, pl.ds(lo * 1024 + 512 + i * 512, 512)].reshape(1024, 512),
+                (((0,), (0,)), ((), ())), preferred_element_type=F32,
+            )
+            owg[1, :, lo, :, pl.ds(i * 512, 512)] = part.reshape(4, 128, 512)
+    owg_b_step, owg_b_total = ring_reduce(
+        y_ring, lambda j: owg.at[1, j], lambda d: ow_far.at[1, d],
+        lambda d, s: ow_full.at[1, d, s],
+    )
+    ow_done()
+
+    def block(i, _):
+        ag[i] = lax.dot_general(
+            ogt[i].reshape(256, 2048), owt[...].reshape(512, 2048),
             (((1,), (1,)), ((), ())), preferred_element_type=F32,
-        ).reshape(4, 2, 64, 512)
-        ig[h, :, :, pl.ds(0, 512)] = part[:, 0]
-        ig[h, :, :, pl.ds(512, 512)] = part[:, 1]
-    ag_sent = send(ig.at[1 - col, :, :, pl.ds(0, 1024)], agr, sibling)
-    qw_step(2)
-    ag_sent.wait()
-    for half in range(2):
-        cols = pl.ds(half * 512, 512)
-        agb[:, pl.ds(half * 64, 64), :] = (ig[col, :, :, cols] + agr[:, :, cols]).astype(BF16)
-    for i in range(4):
-        post(agb.at[:, :, pl.ds(i * 128, 128)], ag_out.at[y], return_ag[i], 6 + y)
-    owg_sum.second()
-    km_step(4)
+        ).reshape(4, 64, 512)
+        return 0
+
+    lax.fori_loop(0, 4, block, 0)
+    ag_sent = [send(ag.at[lo * 2 + 1 - col], agr.at[lo], sibling) for lo in range(2)]
     k_own.wait()
     arrive(k_copies)
     for lo in range(2):
@@ -335,11 +309,20 @@
         high = total.astype(BF16)
         qkt[lo * 2 + col, :, :, pl.ds(512, 128)] = high
         qkt[lo * 2 + col, :, :, pl.ds(640, 128)] = (total - high.astype(F32)).astype(BF16)
-    qw_step(3)
+    km_step(3)
+    owg_a_step(2)
+    arrive(ag_sent)
+    for lo in range(2):
+        agb[lo] = (ag[lo * 2 + col] + agr[lo]).astype(BF16)
+    ag_slot = ag_out.at[y, :, zlo]
+    stored.append(place(agb.at[zlo, :, :, at128(y)], ag_slot))
+    last += [send(agb.at[lo, :, :, at128(j)], ag_slot, to) for j, lo, to in places[1:]]
     q_own.wait()
     arrive(q_copies)
     q_shared = [send(v, v, sibling) for v in [qkt.at[lo * 2 + col] for lo in range(2)]]
-    qw_step(4)
+    owg_b_step(2)
+    qw_step(3)
+    km_step(4)
     li_all.done()
     arrive(q_shared)
 
@@ -357,15 +340,23 @@
             kwg[lo, lax.div(i, 2), pl.ds(lax.rem(i, 2) * 2, 2)] = sums.reshape(2, 128, 128)
             return 0
         lax.fori_loop(0, 4, block, 0)
-    qwg_step, qwg_total = ring_reduce(
-        z_ring, lambda zz: qwg.at[lax.rem(zz, 2), lax.div(zz, 2)],
-        lambda d: qw_far.at[d], lambda d, s: qw_full.at[d, s],
+    qwg_a_step, qwg_a_total = ring_reduce(
+        z_ring,
+        lambda zz: qwg.at[lax.rem(zz, 2), lax.div(zz, 2), pl.ds(0, 512)],
+        lambda d: qw_far.at[0, d], lambda d, s: qw_full.at[0, d, s],
+    )
+    qwg_b_step, qwg_b_total = ring_reduce(
+        z_ring,
+        lambda zz: qwg.at[lax.rem(zz, 2), lax.div(zz, 2), pl.ds(512, 512)],
+        lambda d: qw_far.at[1, d], lambda d, s: qw_full.at[1, d, s],
     )
     kwg_step, kwg_total = ring_reduce(
         z_ring, lambda zz: kwg.at[lax.rem(zz, 2), :, lax.div(zz, 2)],
         lambda d: kw_far.at[d], lambda d, s: kw_full.at[d, s],
     )
 
+    qw_step(4)
+    qwg_a_step(2)
     qw_done()
     km_done()
     for lo in range(2):
@@ -374,58 +365,80 @@
         w3[lo, :, pl.ds(640, 128)] = keys
     for lo in range(2):
         def block(i, _, lo=lo):
-            cols = pl.ds(pl.multiple_of(lo * 1024 + i * 256, 256), 256)
-            rows = pl.ds(pl.multiple_of(i * 256, 256), 256)
+            rows = pl.ds(pl.multiple_of(0 + i * 256, 256), 256)
             part = lax.dot_general(
                 qkt[...].reshape(1024, 768), w3[lo, rows, :],
                 (((1,), (1,)), ((), ())), preferred_element_type=F32,
             )
-            ig[:, :, :, cols] = part.reshape(4, 4, 64, 256)
+            cols = pl.ds(pl.multiple_of(lo * 512 + i * 256, 256), 256)
+            ig[0, :, :, :, cols] = part.reshape(4, 4, 64, 256)
             return 0
-        lax.fori_loop(0, 4, block, 0)
-    ig_sum = Reduce(ig, ig_got)
-
-    qwg_step(2)
-    ig_sum.second()
+        lax.fori_loop(0, 2, block, 0)
+    ig_sum_a = Reduce(ig.at[0], ig_got[0])
+    qwg_b_step(2)
     kwg_step(2)
+    for lo in range(2):
+        def block(i, _, lo=lo):
+            rows = pl.ds(pl.multiple_of(512 + i * 256, 256), 256)
+            part = lax.dot_general(
+                qkt[...].reshape(1024, 768), w3[lo, rows, :],
+                (((1,), (1,)), ((), ())), preferred_element_type=F32,
+            )
+            cols = pl.ds(pl.multiple_of(lo * 512 + i * 256, 256), 256)
+            ig[1, :, :, :, cols] = part.reshape(4, 4, 64, 256)
+            return 0
+        lax.fori_loop(0, 2, block, 0)
+    ig_sum_b = Reduce(ig.at[1], ig_got[1])
+    owg_a_mine = owg_a_total()
+    owg_a_sent = send(owg_a_mine.at[1 - zlo], owy.at[0], zpartner)
+    qwg_a_step(3)
     kwg_step(3)
-    qwg_step(3)
+    ig_sum_a.second()
+    owg_b_mine = owg_b_total()
+    owg_b_sent = send(owg_b_mine.at[1 - zlo], owy.at[1], zpartner)
+    qwg_b_step(3)
+    ig_sum_b.second()
+    ig_sum_a.inner()
+    owg_a_sent.wait_recv()
+    add(owg_a_mine.at[zlo], owy.at[0])
+    stored.append(place(owg_a_mine.at[zlo], owg_out.at[:, pl.ds(0, 512)]))
     kwg_step(4)
-    qwg_step(4)
+    qwg_a_step(4)
     kwg_mine = kwg_total()
     kwg_sent = send(kwg_mine.at[1 - ylo], kwy, ypartner)
-    owg_sum.inner()
-    ig_sum.inner()
+    ig_sum_b.inner()
+    qwg_b_step(4)
     kwg_sent.wait_recv()
     kwy[...] = kwy[...] + kwg_mine[ylo]
-    kwg_own = place(kwy, kwg_out)
-    owg_sum.second()
-    ig_sum.second()
-    qwg_own = place(qwg_total(), qwg_out)
-    owg_sum.total()
-    for b in range(2):
-        post(
-            owg.at[x, y, :, pl.ds(b * 1024, 1024)],
-            owg_out.at[pl.ds(pl.multiple_of(ylo * 64, 64), 64)], return_ow[b], 10 + ylo,
-        )
-    ig_sum.total()
-    fin[...] = ig[x, y].astype(BF16)
-    ig_own = place(fin.at[:, at1024(zlo)], ig_out.at[zlo])
-    ig_sent = send(fin.at[:, at1024(1 - zlo)], ig_out.at[zlo], zpartner)
+    stored.append(place(kwy, kwg_out))
+    ig_sum_a.second()
+    owg_b_sent.wait_recv()
+    add(owg_b_mine.at[zlo], owy.at[1])
+    stored.append(place(owg_b_mine.at[zlo], owg_out.at[:, pl.ds(512, 512)]))
+    ig_sum_b.second()
+    ig_sum_a.total()
+    fin[0] = ig[0, x, y].astype(BF16)
+    cols = pl.ds(0, 512)
+    mine, other = [
+        fin.at[0, :, pl.ds(pl.multiple_of(lo * 512, 512), 512)] for lo in (zlo, 1 - zlo)
+    ]
+    stored.append(place(mine, ig_out.at[zlo, :, cols]))
+    last.append(send(other, ig_out.at[zlo, :, cols], zpartner))
+    stored.append(place(qwg_a_total(), qwg_out.at[pl.ds(0, 512)]))
+    stored.append(place(qwg_b_total(), qwg_out.at[pl.ds(512, 512)]))
+    ig_sum_b.total()
+    fin[1] = ig[1, x, y].astype(BF16)
+    cols = pl.ds(512, 512)
+    mine, other = [
+        fin.at[1, :, pl.ds(pl.multiple_of(lo * 512, 512), 512)] for lo in (zlo, 1 - zlo)
+    ]
+    stored.append(place(mine, ig_out.at[zlo, :, cols]))
+    last.append(send(other, ig_out.at[zlo, :, cols], zpartner))
+    arrive(last)
+    for copy in stored:
+        copy.wait()
     for copy in sent:
-        if copy is not ag_sent:
-            copy.wait_send()
-    for copy, own in guarded:
-        @pl.when(jnp.logical_not(own))
-        def _(copy=copy):
-            copy.wait_send()
-    for j in range(4):
-        collect(ag_out.at[j], 6 + j)
-    for r in range(2):
-        collect(owg_out.at[pl.ds(r * 64, 64)], 10 + r)
-    ig_sent.wait_recv()
-    for copy in (qwg_own, ig_own, kwg_own):
-        copy.wait()
+        copy.wait_send()
 
 
 def finish(*refs):
@@ -435,43 +448,45 @@
 
 def shards(layer_input, attn_out, out_grad, q_grad, k_grad, q_weight, k_weight, o_weight):
     shapes = (
-        ((2, 64, 1024), BF16), ((4, 4, 128, 128), BF16), ((1024, 128), F32),
+        ((2, 64, 1024), BF16), ((4, 4, 2, 64, 128), BF16), ((1024, 128), F32),
         ((128, 128), F32), ((128, 1024), F32),
     )
     vmem = pltpu.VMEM
     def reduction():
         return (
-            vmem((2, 2, 2, 32, 2048), F32), vmem((2, 2, 4, 32, 2048), F32),
-            vmem((2, 2, 16, 2048), F32), vmem((2, 2, 32, 2048), F32),
+            vmem((2, 2, 2, 32, 1024), F32), vmem((2, 2, 4, 32, 1024), F32),
+            vmem((2, 2, 16, 1024), F32), vmem((2, 2, 32, 1024), F32),
         )
 
     scratch = [
         vmem((4, 4, 64, 2048), BF16),
+        vmem((4, 128, 2048), BF16),
         vmem((4, 4, 64, 2048), BF16),
-        vmem((4, 128, 2048), BF16),
         vmem((4, 4, 64, 768), BF16),
-        vmem((2, 4, 128, 512), BF16),
+        vmem((4, 4, 64, 512), BF16),
         vmem((2, 1024, 768), BF16),
         vmem((2, 2, 4, 128, 128), BF16),
         vmem((4, 2, 4, 64, 128), BF16),
-        vmem((4, 4, 64, 2048), F32),
-        vmem((4, 4, 64, 2048), F32),
-        reduction(),
-        reduction(),
+        vmem((2, 4, 4, 64, 1024), F32),
+        vmem((2, 4, 2, 128, 512), F32),
+        tuple(reduction() for _ in range(2)),
+        vmem((2, 2, 1, 128, 512), F32),
+        vmem((2, 2, 1, 2, 128, 512), F32),
+        vmem((2, 128, 512), F32),
         vmem((2, 4, 1024, 128), F32),
         vmem((2, 2, 4, 128, 128), F32),
-        vmem((2, 512, 128), F32),
-        vmem((2, 3, 1024, 128), F32),
+        vmem((2, 2, 256, 128), F32),
+        vmem((2, 2, 3, 512, 128), F32),
         vmem((2, 1, 128, 128), F32),
         vmem((2, 3, 2, 128, 128), F32),
         vmem((128, 128), F32),
-        vmem((4, 64, 1024), F32),
-        vmem((4, 128, 512), BF16),
-        vmem((64, 2048), BF16),
+        vmem((4, 4, 64, 512), F32),
+        vmem((2, 4, 64, 512), F32),
+        vmem((2, 4, 64, 512), BF16),
+        vmem((2, 64, 1024), BF16),
         pltpu.SemaphoreType.DMA((COPIES,)),
         pltpu.SemaphoreType.DMA((COPIES,)),
-        pltpu.SemaphoreType.DMA((16,)),
-        pltpu.SemaphoreType.DMA((32,)),
+        pltpu.SemaphoreType.DMA((24,)),
     ]
     ig, ag, qwg, kwg, owg = pl.pallas_call(
         kernel,
@@ -485,8 +500,8 @@
         cost_estimate=pl.CostEstimate(flops=14 * 10**9, bytes_accessed=5 * 10**6, transcendentals=0),
     )(
         layer_input.reshape(2, 64, 1024),
-        attn_out.reshape(4, 4, 128, 128),
-        out_grad,
+        attn_out.reshape(4, 4, 2, 64, 128),
+        out_grad.reshape(2, 64, 1024),
         q_grad.reshape(4, 8, 64, 128),
         k_grad.reshape(4, 8, 64, 128),
         q_weight,

time: 191 us -> 181 us (0.948)
  Pallas kernels: 189 us -> 180 us
    pallas_call x1, Pallas kernels: 187 us -> 177 us  [shards(): pl.pallas_call(kernel, out_shape=[jax.ShapeDtypeStruct(*shape) for shape...]
where the time goes in v5:
time: 181 us; the launch traced here: 180 us
  Pallas kernels  180 us (99%)
    pallas_call x1, Pallas kernels, shards(): pl.pallas_call(kernel, out_shape=[jax.ShapeDtypeStruct(*shape) for shape...  177 us

profile of v5, /device:TPU:2, one launch (start us, length us, event | category | flops | bytes accessed | tf_op | source)
XLA Modules:
  0.0 180.4 jit_solution(18145893801219648858)
XLA Ops:
  0.6 177.0 %shard_map.119 = (bf16[2,64,1024]{2,1,0:T(8,128)(2,1)}, bf16[4,4,2,64,128]{4,3,2,1,0:T(8,128)(2,1)}, f32[1024,128]{1,0:T(8,128)}, f32[128,128]{1,0:T(8,128)}, f32[128,1024]{1,0:T(8,128)}) custom-call(bf16[2,64,1024]{2,1,0:T(8,128)(2,1)} %bitcast.14, bf16[4,4,2,64,128]{4,3,2,1,0:T(8,128)(2,1)} %bitcast.11, bf16[2,64,1024]{2,1,0:T(8,128)(2,1)} %bitcast.15, ...), custom_call_target="tpu_custom_call" | custom-call | flops 14000000000 | bytes 5000000 | tf_op jit(solution)/shard_map/pallas_call | solution.py:491
  177.6 2.7 %shard_map.120 = (bf16[128,1024]{1,0:T(8,128)(2,1)}, bf16[2048,128]{1,0:T(8,128)(2,1)}, f32[1024,128]{1,0:T(8,128)}, f32[128,128]{1,0:T(8,128)}, f32[128,1024]{1,0:T(8,128)}) custom-call(bf16[128,1024]{1,0:T(8,128)(2,1)} %bitcast.10, bf16[2048,128]{1,0:T(8,128)(2,1)} %bitcast.9, f32[1024,128]{1,0:T(8,128)} %get-tuple-element.17.refs_2_, ...), custom_call_target="tpu_custom_call" | custom-call | tf_op jit(solution)/shard_map/pallas_call | solution.py:512

commit v6 on v5

--- a/solution.py
+++ b/solution.py
@@ -52,6 +52,8 @@
     x_ring = (4, x, device(-1, 0, 0), device(1, 0, 0))
     y_ring = (4, y, device(0, -1, 0), device(0, 1, 0))
     z_ring = (8, z, device(0, 0, -1), device(0, 0, 1))
+    odd = zlo == 1
+    across = device(0, 0, 2 * zlo - 1)
 
     zh_ring = (4, zh, device(0, 0, -2), device(0, 0, 2))
 
@@ -111,6 +113,10 @@
         def step(s):
             arrive(steps[-1])
             half = s == n // 2
+            if half and n == 8:
+                far = piece(lax.select(odd, rem(me - 3, n), rem(me + 3, n)), None)
+                steps.append([send(far, far, across)])
+                return
             a = piece(rem(me + s - 1, n), 0 if half else None)
             b = piece(rem(me - s + 1, n), 1 if half else None)
             steps.append([send(a, a, left), send(b, b, right)])
@@ -122,15 +128,21 @@
         size = far(0).shape[0]
         halves = [pl.ds(0, size), pl.ds(size, size)]
         last = n // 2
-        across = piece(rem(me + last, n))
-        steps = [[
-            send(across.at[halves[0]], far(0), left), send(across.at[halves[1]], far(1), right)
-        ]]
+        opposite = piece(rem(me + last, n))
+        if n == 8:
+            steps = [[send(opposite, far(0), across)]]
+        else:
+            steps = [[
+                send(opposite.at[halves[0]], far(0), left),
+                send(opposite.at[halves[1]], far(1), right),
+            ]]
 
         def step(s):
             arrive(steps[-1])
             a, b = piece(rem(me - (last + 1 - s), n)), piece(rem(me + (last + 1 - s), n))
-            if s == 2:
+            if s == 2 and n == 8:
+                add(piece(lax.select(odd, rem(me - 3, n), rem(me + 3, n))), far(0))
+            elif s == 2:
                 add(a.at[halves[0]], far(0))
                 add(b.at[halves[1]], far(1))
             else:
@@ -222,9 +234,9 @@
     og_slot = ogt.at[x, zh, :, at1024(zlo)]
     og_own = place(og.at[zlo], og_slot)
     og_sent = send(og.at[1 - zlo], og_slot, zpartner)
+    qw_own = place(qw, qw_slot(z, None))
     km_own = place(kw, km.at[zlo, ylo, zh])
     km_sent = send(kw, km.at[zlo, ylo, zh], ypartner)
-    qw_own = place(qw, qw_slot(z, None))
     li_slot = lit.at[x, y, :, at1024(zlo)]
     li_own = place(li.at[zlo], li_slot)
     li_sent = send(li.at[1 - zlo], li_slot, zpartner)
@@ -236,31 +248,32 @@
     li_all = Gather(lit)
     li_all.inner()
     li_all.outer()
+    km_own.wait()
+    km_sent.wait_recv()
+    km_step, km_done = ring_gather(z_ring, km_slot)
     og_step(2)
     og_done()
     og_step, og_done = ring_gather(x_ring, lambda i, h: ogt.at[i, part_of(4, h)])
+    ow_slot = owt.at[y, :, at1024(zlo)]
+    ow_own = place(ow, ow_slot)
+    ow_sent = send(ow, ow_slot, zpartner)
+    qw_own.wait()
+    qw_step, qw_done = ring_gather(z_ring, qw_slot)
     ao_slot = aot.at[quarter, :, :, at128(y)]
     ao_own = place(ao.at[y, :, zlo], ao_slot)
     ao_copies = [send(ao.at[j, :, lo], ao_slot, to) for j, lo, to in places[1:]]
-    km_own.wait()
-    km_sent.wait_recv()
-    km_step, km_done = ring_gather(z_ring, km_slot)
-    ow_slot = owt.at[y, :, at1024(zlo)]
-    ow_own = place(ow, ow_slot)
-    ow_sent = send(ow, ow_slot, zpartner)
+    ow_own.wait()
+    ow_sent.wait_recv()
+    ow_step, ow_done = ring_gather(y_ring, lambda j, h: owt.at[j, part_of(128, h)])
+    k_own, k_copies = spread(k, kbuf.at[zh, zlo])
+    qw_step(2)
+    og_step(2)
+    km_step(2)
+    q_own, q_copies = spread(q, qkt.at[quarter, :, :, at128(zh)])
     ao_own.wait()
     arrive(ao_copies)
     ao_shared = [send(v, v, sibling) for v in [aot.at[lo * 2 + col] for lo in range(2)]]
-    k_own, k_copies = spread(k, kbuf.at[zh, zlo])
-    ow_own.wait()
-    ow_sent.wait_recv()
-    ow_step, ow_done = ring_gather(y_ring, lambda j, h: owt.at[j, part_of(128, h)])
-    og_step(2)
-    qw_own.wait()
-    qw_step, qw_done = ring_gather(z_ring, qw_slot)
     ow_step(2)
-    q_own, q_copies = spread(q, qkt.at[quarter, :, :, at128(zh)])
-    km_step(2)
     li_all.inner()
     og_done()
     arrive(ao_shared)
@@ -276,7 +289,6 @@
         y_ring, lambda j: owg.at[0, j], lambda d: ow_far.at[0, d],
         lambda d, s: ow_full.at[0, d, s],
     )
-    qw_step(2)
     for lo in range(2):
         for i in range(1):
             part = lax.dot_general(
@@ -289,6 +301,7 @@
         y_ring, lambda j: owg.at[1, j], lambda d: ow_far.at[1, d],
         lambda d, s: ow_full.at[1, d, s],
     )
+    qw_step(3)
     ow_done()
 
     def block(i, _):
@@ -311,17 +324,16 @@
         qkt[lo * 2 + col, :, :, pl.ds(640, 128)] = (total - high.astype(F32)).astype(BF16)
     km_step(3)
     owg_a_step(2)
+    q_own.wait()
+    arrive(q_copies)
+    q_shared = [send(v, v, sibling) for v in [qkt.at[lo * 2 + col] for lo in range(2)]]
+    qw_step(4)
     arrive(ag_sent)
     for lo in range(2):
         agb[lo] = (ag[lo * 2 + col] + agr[lo]).astype(BF16)
     ag_slot = ag_out.at[y, :, zlo]
     stored.append(place(agb.at[zlo, :, :, at128(y)], ag_slot))
     last += [send(agb.at[lo, :, :, at128(j)], ag_slot, to) for j, lo, to in places[1:]]
-    q_own.wait()
-    arrive(q_copies)
-    q_shared = [send(v, v, sibling) for v in [qkt.at[lo * 2 + col] for lo in range(2)]]
-    owg_b_step(2)
-    qw_step(3)
     km_step(4)
     li_all.done()
     arrive(q_shared)
@@ -340,23 +352,16 @@
             kwg[lo, lax.div(i, 2), pl.ds(lax.rem(i, 2) * 2, 2)] = sums.reshape(2, 128, 128)
             return 0
         lax.fori_loop(0, 4, block, 0)
-    qwg_a_step, qwg_a_total = ring_reduce(
+    qwg_step, qwg_total = ring_reduce(
         z_ring,
-        lambda zz: qwg.at[lax.rem(zz, 2), lax.div(zz, 2), pl.ds(0, 512)],
+        lambda zz: qwg.at[lax.rem(zz, 2), lax.div(zz, 2), pl.ds(0, 1024)],
         lambda d: qw_far.at[0, d], lambda d, s: qw_full.at[0, d, s],
-    )
-    qwg_b_step, qwg_b_total = ring_reduce(
-        z_ring,
-        lambda zz: qwg.at[lax.rem(zz, 2), lax.div(zz, 2), pl.ds(512, 512)],
-        lambda d: qw_far.at[1, d], lambda d, s: qw_full.at[1, d, s],
     )
     kwg_step, kwg_total = ring_reduce(
         z_ring, lambda zz: kwg.at[lax.rem(zz, 2), :, lax.div(zz, 2)],
         lambda d: kw_far.at[d], lambda d, s: kw_full.at[d, s],
     )
 
-    qw_step(4)
-    qwg_a_step(2)
     qw_done()
     km_done()
     for lo in range(2):
@@ -375,8 +380,9 @@
             return 0
         lax.fori_loop(0, 2, block, 0)
     ig_sum_a = Reduce(ig.at[0], ig_got[0])
-    qwg_b_step(2)
-    kwg_step(2)
+    owg_a_mine = owg_a_total()
+    owg_a_sent = send(owg_a_mine.at[1 - zlo], owy.at[0], zpartner)
+    owg_b_step(2)
     for lo in range(2):
         def block(i, _, lo=lo):
             rows = pl.ds(pl.multiple_of(512 + i * 256, 256), 256)
@@ -389,33 +395,28 @@
             return 0
         lax.fori_loop(0, 2, block, 0)
     ig_sum_b = Reduce(ig.at[1], ig_got[1])
-    owg_a_mine = owg_a_total()
-    owg_a_sent = send(owg_a_mine.at[1 - zlo], owy.at[0], zpartner)
-    qwg_a_step(3)
+    kwg_step(2)
+    ig_sum_a.second()
+    qwg_step(2)
     kwg_step(3)
-    ig_sum_a.second()
-    owg_b_mine = owg_b_total()
-    owg_b_sent = send(owg_b_mine.at[1 - zlo], owy.at[1], zpartner)
-    qwg_b_step(3)
+    qwg_step(3)
     ig_sum_b.second()
-    ig_sum_a.inner()
+    kwg_step(4)
     owg_a_sent.wait_recv()
     add(owg_a_mine.at[zlo], owy.at[0])
     stored.append(place(owg_a_mine.at[zlo], owg_out.at[:, pl.ds(0, 512)]))
-    kwg_step(4)
-    qwg_a_step(4)
+    owg_b_mine = owg_b_total()
+    owg_b_sent = send(owg_b_mine.at[1 - zlo], owy.at[1], zpartner)
+    qwg_step(4)
+    ig_sum_a.inner()
     kwg_mine = kwg_total()
     kwg_sent = send(kwg_mine.at[1 - ylo], kwy, ypartner)
     ig_sum_b.inner()
-    qwg_b_step(4)
+    ig_sum_a.second()
+    ig_sum_b.second()
     kwg_sent.wait_recv()
     kwy[...] = kwy[...] + kwg_mine[ylo]
     stored.append(place(kwy, kwg_out))
-    ig_sum_a.second()
-    owg_b_sent.wait_recv()
-    add(owg_b_mine.at[zlo], owy.at[1])
-    stored.append(place(owg_b_mine.at[zlo], owg_out.at[:, pl.ds(512, 512)]))
-    ig_sum_b.second()
     ig_sum_a.total()
     fin[0] = ig[0, x, y].astype(BF16)
     cols = pl.ds(0, 512)
@@ -424,8 +425,9 @@
     ]
     stored.append(place(mine, ig_out.at[zlo, :, cols]))
     last.append(send(other, ig_out.at[zlo, :, cols], zpartner))
-    stored.append(place(qwg_a_total(), qwg_out.at[pl.ds(0, 512)]))
-    stored.append(place(qwg_b_total(), qwg_out.at[pl.ds(512, 512)]))
+    owg_b_sent.wait_recv()
+    add(owg_b_mine.at[zlo], owy.at[1])
+    stored.append(place(owg_b_mine.at[zlo], owg_out.at[:, pl.ds(512, 512)]))
     ig_sum_b.total()
     fin[1] = ig[1, x, y].astype(BF16)
     cols = pl.ds(512, 512)
@@ -434,6 +436,7 @@
     ]
     stored.append(place(mine, ig_out.at[zlo, :, cols]))
     last.append(send(other, ig_out.at[zlo, :, cols], zpartner))
+    stored.append(place(qwg_total(), qwg_out.at[pl.ds(0, 1024)]))
     arrive(last)
     for copy in stored:
         copy.wait()
@@ -475,9 +478,9 @@
         vmem((2, 128, 512), F32),
         vmem((2, 4, 1024, 128), F32),
         vmem((2, 2, 4, 128, 128), F32),
-        vmem((2, 2, 256, 128), F32),
-        vmem((2, 2, 3, 512, 128), F32),
-        vmem((2, 1, 128, 128), F32),
+        vmem((1, 1, 1024, 128), F32),
+        vmem((1, 2, 3, 1024, 128), F32),
+        vmem((1, 2, 128, 128), F32),
         vmem((2, 3, 2, 128, 128), F32),
         vmem((128, 128), F32),
         vmem((4, 4, 64, 512), F32),

time: 181 us -> 172 us (0.950)
  Pallas kernels: 180 us -> 171 us
    pallas_call x1, Pallas kernels: 177 us -> 169 us  [shards(): pl.pallas_call(kernel, out_shape=[jax.ShapeDtypeStruct(*shape) for shape...]
where the time goes in v6:
time: 172 us
  Pallas kernels  171 us (99%)
    pallas_call x1, Pallas kernels, shards(): pl.pallas_call(kernel, out_shape=[jax.ShapeDtypeStruct(*shape) for shape...  169 us

profile of v6, /device:TPU:2, one launch (start us, length us, event | category | flops | bytes accessed | tf_op | source)
XLA Modules:
  0.0 172.1 jit_solution(4297539462210633415)
XLA Ops:
  0.6 168.7 %shard_map.119 = (bf16[2,64,1024]{2,1,0:T(8,128)(2,1)}, bf16[4,4,2,64,128]{4,3,2,1,0:T(8,128)(2,1)}, f32[1024,128]{1,0:T(8,128)}, f32[128,128]{1,0:T(8,128)}, f32[128,1024]{1,0:T(8,128)}) custom-call(bf16[2,64,1024]{2,1,0:T(8,128)(2,1)} %bitcast.14, bf16[4,4,2,64,128]{4,3,2,1,0:T(8,128)(2,1)} %bitcast.11, bf16[2,64,1024]{2,1,0:T(8,128)(2,1)} %bitcast.15, ...), custom_call_target="tpu_custom_call" | custom-call | flops 14000000000 | bytes 5000000 | tf_op jit(solution)/shard_map/pallas_call | solution.py:494
  169.4 2.7 %shard_map.120 = (bf16[128,1024]{1,0:T(8,128)(2,1)}, bf16[2048,128]{1,0:T(8,128)(2,1)}, f32[1024,128]{1,0:T(8,128)}, f32[128,128]{1,0:T(8,128)}, f32[128,1024]{1,0:T(8,128)}) custom-call(bf16[128,1024]{1,0:T(8,128)(2,1)} %bitcast.10, bf16[2048,128]{1,0:T(8,128)(2,1)} %bitcast.9, f32[1024,128]{1,0:T(8,128)} %get-tuple-element.17.refs_2_, ...), custom_call_target="tpu_custom_call" | custom-call | tf_op jit(solution)/shard_map/pallas_call | solution.py:515

commit v7 on v6

--- a/solution.py
+++ b/solution.py
@@ -225,63 +225,82 @@
         ]
         return place(src.at[:, z], slot), copies
 
-    def qw_slot(zz, half):
-        return w3.at[lax.rem(zz, 2), part_of(1024, half), at128(lax.div(zz, 2))]
+    def half_of(lo):
+        return pl.ds(pl.multiple_of(lo * 512, 512), 512)
+
+    def qw_slot(c):
+        def slot(zz, half):
+            rows = pl.ds(c * 512, 512) if half is None else pl.ds(c * 512 + half * 256, 256)
+            return w3.at[lax.rem(zz, 2), rows, at128(lax.div(zz, 2))]
+        return slot
 
     def km_slot(zz, half):
         return km.at[lax.rem(zz, 2), part_of(2, half), lax.div(zz, 2)]
 
-    og_slot = ogt.at[x, zh, :, at1024(zlo)]
-    og_own = place(og.at[zlo], og_slot)
-    og_sent = send(og.at[1 - zlo], og_slot, zpartner)
-    qw_own = place(qw, qw_slot(z, None))
-    km_own = place(kw, km.at[zlo, ylo, zh])
-    km_sent = send(kw, km.at[zlo, ylo, zh], ypartner)
     li_slot = lit.at[x, y, :, at1024(zlo)]
     li_own = place(li.at[zlo], li_slot)
     li_sent = send(li.at[1 - zlo], li_slot, zpartner)
-    og_own.wait()
-    og_sent.wait_recv()
-    og_step, og_done = ring_gather(zh_ring, lambda i, h: ogt.at[x, i, part_of(64, h)])
+    og_a_slot = ogt.at[0, x, zh, :, half_of(zlo)]
+    og_a_own = place(og.at[zlo, :, pl.ds(0, 512)], og_a_slot)
+    og_a_sent = send(og.at[1 - zlo, :, pl.ds(0, 512)], og_a_slot, zpartner)
+    qw_b_own = place(qw.at[pl.ds(512, 512)], qw_slot(1)(z, None))
+    km_own = place(kw, km.at[zlo, ylo, zh])
+    km_sent = send(kw, km.at[zlo, ylo, zh], ypartner)
+    km_own.wait()
+    km_sent.wait_recv()
+    km_step, km_done = ring_gather(z_ring, km_slot)
+    og_b_slot = ogt.at[1, x, zh, :, half_of(zlo)]
+    og_b_own = place(og.at[zlo, :, pl.ds(512, 512)], og_b_slot)
+    og_b_sent = send(og.at[1 - zlo, :, pl.ds(512, 512)], og_b_slot, zpartner)
     li_own.wait()
     li_sent.wait_recv()
     li_all = Gather(lit)
+    qw_a_own = place(qw.at[pl.ds(0, 512)], qw_slot(0)(z, None))
+    og_a_own.wait()
+    og_a_sent.wait_recv()
+    og_a_step, og_a_done = ring_gather(
+        zh_ring, lambda i, h: ogt.at[0, x, i, part_of(64, h)]
+    )
     li_all.inner()
+    ao_slot = aot.at[quarter, :, :, at128(y)]
+    ao_own = place(ao.at[y, :, zlo], ao_slot)
+    ao_copies = [send(ao.at[j, :, lo], ao_slot, to) for j, lo, to in places[1:]]
     li_all.outer()
-    km_own.wait()
-    km_sent.wait_recv()
-    km_step, km_done = ring_gather(z_ring, km_slot)
-    og_step(2)
-    og_done()
-    og_step, og_done = ring_gather(x_ring, lambda i, h: ogt.at[i, part_of(4, h)])
+    og_a_step(2)
     ow_slot = owt.at[y, :, at1024(zlo)]
     ow_own = place(ow, ow_slot)
     ow_sent = send(ow, ow_slot, zpartner)
-    qw_own.wait()
-    qw_step, qw_done = ring_gather(z_ring, qw_slot)
-    ao_slot = aot.at[quarter, :, :, at128(y)]
-    ao_own = place(ao.at[y, :, zlo], ao_slot)
-    ao_copies = [send(ao.at[j, :, lo], ao_slot, to) for j, lo, to in places[1:]]
+    og_a_done()
+    og_a_step, og_a_done = ring_gather(x_ring, lambda i, h: ogt.at[0, i, part_of(4, h)])
+    og_b_own.wait()
+    og_b_sent.wait_recv()
+    og_b_step, og_b_done = ring_gather(
+        zh_ring, lambda i, h: ogt.at[1, x, i, part_of(64, h)]
+    )
+    qw_a_own.wait()
+    qw_a_step, qw_a_done = ring_gather(z_ring, qw_slot(0))
     ow_own.wait()
     ow_sent.wait_recv()
     ow_step, ow_done = ring_gather(y_ring, lambda j, h: owt.at[j, part_of(128, h)])
-    k_own, k_copies = spread(k, kbuf.at[zh, zlo])
-    qw_step(2)
-    og_step(2)
+    og_b_step(2)
     km_step(2)
     q_own, q_copies = spread(q, qkt.at[quarter, :, :, at128(zh)])
     ao_own.wait()
     arrive(ao_copies)
     ao_shared = [send(v, v, sibling) for v in [aot.at[lo * 2 + col] for lo in range(2)]]
+    og_a_step(2)
     ow_step(2)
-    li_all.inner()
-    og_done()
+    og_b_done()
+    og_b_step, og_b_done = ring_gather(x_ring, lambda i, h: ogt.at[1, i, part_of(4, h)])
+    qw_b_own.wait()
+    qw_b_step, qw_b_done = ring_gather(z_ring, qw_slot(1))
+    og_a_done()
     arrive(ao_shared)
     for lo in range(2):
         for i in range(1):
             part = lax.dot_general(
                 aot[...].reshape(1024, 512),
-                ogt[:, :, :, pl.ds(lo * 1024 + 0 + i * 512, 512)].reshape(1024, 512),
+                ogt[0, :, :, :, pl.ds(lo * 512 + i * 512, 512)].reshape(1024, 512),
                 (((0,), (0,)), ((), ())), preferred_element_type=F32,
             )
             owg[0, :, lo, :, pl.ds(i * 512, 512)] = part.reshape(4, 128, 512)
@@ -289,11 +308,18 @@
         y_ring, lambda j: owg.at[0, j], lambda d: ow_far.at[0, d],
         lambda d, s: ow_full.at[0, d, s],
     )
+    qw_a_step(2)
+    km_step(3)
+    k_own, k_copies = spread(k, kbuf.at[zh, zlo])
+    qw_b_step(2)
+    owg_a_step(2)
+    og_b_step(2)
+    og_b_done()
     for lo in range(2):
         for i in range(1):
             part = lax.dot_general(
                 aot[...].reshape(1024, 512),
-                ogt[:, :, :, pl.ds(lo * 1024 + 512 + i * 512, 512)].reshape(1024, 512),
+                ogt[1, :, :, :, pl.ds(lo * 512 + i * 512, 512)].reshape(1024, 512),
                 (((0,), (0,)), ((), ())), preferred_element_type=F32,
             )
             owg[1, :, lo, :, pl.ds(i * 512, 512)] = part.reshape(4, 128, 512)
@@ -301,18 +327,25 @@
         y_ring, lambda j: owg.at[1, j], lambda d: ow_far.at[1, d],
         lambda d, s: ow_full.at[1, d, s],
     )
-    qw_step(3)
     ow_done()
 
     def block(i, _):
-        ag[i] = lax.dot_general(
-            ogt[i].reshape(256, 2048), owt[...].reshape(512, 2048),
-            (((1,), (1,)), ((), ())), preferred_element_type=F32,
-        ).reshape(4, 64, 512)
+        total = jnp.zeros((256, 512), F32)
+        for c in range(2):
+            for lo in range(2):
+                total = total + lax.dot_general(
+                    ogt[c, i, :, :, pl.ds(lo * 512, 512)].reshape(256, 512),
+                    owt[:, :, pl.ds(lo * 1024 + c * 512, 512)].reshape(512, 512),
+                    (((1,), (1,)), ((), ())), preferred_element_type=F32,
+                )
+        ag[i] = total.reshape(4, 64, 512)
         return 0
 
     lax.fori_loop(0, 4, block, 0)
     ag_sent = [send(ag.at[lo * 2 + 1 - col], agr.at[lo], sibling) for lo in range(2)]
+    li_all.inner()
+    qw_a_step(3)
+    qw_b_step(3)
     k_own.wait()
     arrive(k_copies)
     for lo in range(2):
@@ -322,19 +355,15 @@
         high = total.astype(BF16)
         qkt[lo * 2 + col, :, :, pl.ds(512, 128)] = high
         qkt[lo * 2 + col, :, :, pl.ds(640, 128)] = (total - high.astype(F32)).astype(BF16)
-    km_step(3)
-    owg_a_step(2)
     q_own.wait()
     arrive(q_copies)
     q_shared = [send(v, v, sibling) for v in [qkt.at[lo * 2 + col] for lo in range(2)]]
-    qw_step(4)
-    arrive(ag_sent)
-    for lo in range(2):
-        agb[lo] = (ag[lo * 2 + col] + agr[lo]).astype(BF16)
-    ag_slot = ag_out.at[y, :, zlo]
-    stored.append(place(agb.at[zlo, :, :, at128(y)], ag_slot))
-    last += [send(agb.at[lo, :, :, at128(j)], ag_slot, to) for j, lo, to in places[1:]]
+    owg_b_step(2)
+    owg_a_mine = owg_a_total()
+    owg_a_sent = send(owg_a_mine.at[1 - zlo], owy.at[0], zpartner)
     km_step(4)
+    qw_a_step(4)
+    qw_b_step(4)
     li_all.done()
     arrive(q_shared)
 
@@ -352,17 +381,28 @@
             kwg[lo, lax.div(i, 2), pl.ds(lax.rem(i, 2) * 2, 2)] = sums.reshape(2, 128, 128)
             return 0
         lax.fori_loop(0, 4, block, 0)
-    qwg_step, qwg_total = ring_reduce(
+    qwg_a_step, qwg_a_total = ring_reduce(
         z_ring,
-        lambda zz: qwg.at[lax.rem(zz, 2), lax.div(zz, 2), pl.ds(0, 1024)],
+        lambda zz: qwg.at[lax.rem(zz, 2), lax.div(zz, 2), pl.ds(0, 512)],
         lambda d: qw_far.at[0, d], lambda d, s: qw_full.at[0, d, s],
+    )
+    qwg_b_step, qwg_b_total = ring_reduce(
+        z_ring,
+        lambda zz: qwg.at[lax.rem(zz, 2), lax.div(zz, 2), pl.ds(512, 512)],
+        lambda d: qw_far.at[1, d], lambda d, s: qw_full.at[1, d, s],
     )
     kwg_step, kwg_total = ring_reduce(
         z_ring, lambda zz: kwg.at[lax.rem(zz, 2), :, lax.div(zz, 2)],
         lambda d: kw_far.at[d], lambda d, s: kw_full.at[d, s],
     )
 
-    qw_done()
+    arrive(ag_sent)
+    for lo in range(2):
+        agb[lo] = (ag[lo * 2 + col] + agr[lo]).astype(BF16)
+    ag_slot = ag_out.at[y, :, zlo]
+    stored.append(place(agb.at[zlo, :, :, at128(y)], ag_slot))
+    last += [send(agb.at[lo, :, :, at128(j)], ag_slot, to) for j, lo, to in places[1:]]
+    qw_a_done()
     km_done()
     for lo in range(2):
         keys = km[lo].reshape(1024, 128)
@@ -380,9 +420,9 @@
             return 0
         lax.fori_loop(0, 2, block, 0)
     ig_sum_a = Reduce(ig.at[0], ig_got[0])
-    owg_a_mine = owg_a_total()
-    owg_a_sent = send(owg_a_mine.at[1 - zlo], owy.at[0], zpartner)
-    owg_b_step(2)
+    owg_b_mine = owg_b_total()
+    owg_b_sent = send(owg_b_mine.at[1 - zlo], owy.at[1], zpartner)
+    qw_b_done()
     for lo in range(2):
         def block(i, _, lo=lo):
             rows = pl.ds(pl.multiple_of(512 + i * 256, 256), 256)
@@ -395,24 +435,28 @@
             return 0
         lax.fori_loop(0, 2, block, 0)
     ig_sum_b = Reduce(ig.at[1], ig_got[1])
+    qwg_b_step(2)
     kwg_step(2)
+    owg_b_sent.wait_recv()
+    add(owg_b_mine.at[zlo], owy.at[1])
+    stored.append(place(owg_b_mine.at[zlo], owg_out.at[:, pl.ds(512, 512)]))
     ig_sum_a.second()
-    qwg_step(2)
+    qwg_a_step(2)
     kwg_step(3)
-    qwg_step(3)
     ig_sum_b.second()
+    qwg_b_step(3)
     kwg_step(4)
+    qwg_a_step(3)
+    qwg_b_step(4)
+    ig_sum_a.inner()
     owg_a_sent.wait_recv()
     add(owg_a_mine.at[zlo], owy.at[0])
     stored.append(place(owg_a_mine.at[zlo], owg_out.at[:, pl.ds(0, 512)]))
-    owg_b_mine = owg_b_total()
-    owg_b_sent = send(owg_b_mine.at[1 - zlo], owy.at[1], zpartner)
-    qwg_step(4)
-    ig_sum_a.inner()
     kwg_mine = kwg_total()
     kwg_sent = send(kwg_mine.at[1 - ylo], kwy, ypartner)
     ig_sum_b.inner()
     ig_sum_a.second()
+    qwg_a_step(4)
     ig_sum_b.second()
     kwg_sent.wait_recv()
     kwy[...] = kwy[...] + kwg_mine[ylo]
@@ -425,9 +469,6 @@
     ]
     stored.append(place(mine, ig_out.at[zlo, :, cols]))
     last.append(send(other, ig_out.at[zlo, :, cols], zpartner))
-    owg_b_sent.wait_recv()
-    add(owg_b_mine.at[zlo], owy.at[1])
-    stored.append(place(owg_b_mine.at[zlo], owg_out.at[:, pl.ds(512, 512)]))
     ig_sum_b.total()
     fin[1] = ig[1, x, y].astype(BF16)
     cols = pl.ds(512, 512)
@@ -436,7 +477,8 @@
     ]
     stored.append(place(mine, ig_out.at[zlo, :, cols]))
     last.append(send(other, ig_out.at[zlo, :, cols], zpartner))
-    stored.append(place(qwg_total(), qwg_out.at[pl.ds(0, 1024)]))
+    stored.append(place(qwg_a_total(), qwg_out.at[pl.ds(0, 512)]))
+    stored.append(place(qwg_b_total(), qwg_out.at[pl.ds(512, 512)]))
     arrive(last)
     for copy in stored:
         copy.wait()
@@ -464,7 +506,7 @@
     scratch = [
         vmem((4, 4, 64, 2048), BF16),
         vmem((4, 128, 2048), BF16),
-        vmem((4, 4, 64, 2048), BF16),
+        vmem((2, 4, 4, 64, 1024), BF16),
         vmem((4, 4, 64, 768), BF16),
         vmem((4, 4, 64, 512), BF16),
         vmem((2, 1024, 768), BF16),
@@ -478,8 +520,8 @@
         vmem((2, 128, 512), F32),
         vmem((2, 4, 1024, 128), F32),
         vmem((2, 2, 4, 128, 128), F32),
-        vmem((1, 1, 1024, 128), F32),
-        vmem((1, 2, 3, 1024, 128), F32),
+        vmem((2, 1, 512, 128), F32),
+        vmem((2, 2, 3, 512, 128), F32),
         vmem((1, 2, 128, 128), F32),
         vmem((2, 3, 2, 128, 128), F32),
         vmem((128, 128), F32),

time: 172 us -> 160 us (0.930)
  Pallas kernels: 171 us -> 159 us
    pallas_call x1, Pallas kernels: 169 us -> 157 us  [shards(): pl.pallas_call(kernel, out_shape=[jax.ShapeDtypeStruct(*shape) for shape...]
where the time goes in v7:
time: 160 us
  Pallas kernels  159 us (99%)
    pallas_call x1, Pallas kernels, shards(): pl.pallas_call(kernel, out_shape=[jax.ShapeDtypeStruct(*shape) for shape...  157 us

profile of v7, /device:TPU:2, one launch (start us, length us, event | category | flops | bytes accessed | tf_op | source)
XLA Modules:
  0.0 159.9 jit_solution(11650758661903386897)
XLA Ops:
  0.6 156.5 %shard_map.119 = (bf16[2,64,1024]{2,1,0:T(8,128)(2,1)}, bf16[4,4,2,64,128]{4,3,2,1,0:T(8,128)(2,1)}, f32[1024,128]{1,0:T(8,128)}, f32[128,128]{1,0:T(8,128)}, f32[128,1024]{1,0:T(8,128)}) custom-call(bf16[2,64,1024]{2,1,0:T(8,128)(2,1)} %bitcast.14, bf16[4,4,2,64,128]{4,3,2,1,0:T(8,128)(2,1)} %bitcast.11, bf16[2,64,1024]{2,1,0:T(8,128)(2,1)} %bitcast.15, ...), custom_call_target="tpu_custom_call" | custom-call | flops 14000000000 | bytes 5000000 | tf_op jit(solution)/shard_map/pallas_call | solution.py:536
  157.2 2.7 %shard_map.120 = (bf16[128,1024]{1,0:T(8,128)(2,1)}, bf16[2048,128]{1,0:T(8,128)(2,1)}, f32[1024,128]{1,0:T(8,128)}, f32[128,128]{1,0:T(8,128)}, f32[128,1024]{1,0:T(8,128)}) custom-call(bf16[128,1024]{1,0:T(8,128)(2,1)} %bitcast.10, bf16[2048,128]{1,0:T(8,128)(2,1)} %bitcast.9, f32[1024,128]{1,0:T(8,128)} %get-tuple-element.17.refs_2_, ...), custom_call_target="tpu_custom_call" | custom-call | tf_op jit(solution)/shard_map/pallas_call | solution.py:557

commit v8 on v7

--- a/solution.py
+++ b/solution.py
@@ -111,15 +111,18 @@
         steps = [[send(own, own, left), send(own, own, right)]]
 
         def step(s):
-            arrive(steps[-1])
             half = s == n // 2
             if half and n == 8:
+                arrive(steps[-1])
                 far = piece(lax.select(odd, rem(me - 3, n), rem(me + 3, n)), None)
                 steps.append([send(far, far, across)])
                 return
             a = piece(rem(me + s - 1, n), 0 if half else None)
             b = piece(rem(me - s + 1, n), 1 if half else None)
-            steps.append([send(a, a, left), send(b, b, right)])
+            steps[-1][0].wait_recv()
+            first = send(a, a, left)
+            steps[-1][1].wait_recv()
+            steps.append([first, send(b, b, right)])
 
         return step, lambda: arrive(steps[-1])
 
@@ -138,17 +141,22 @@
             ]]
 
         def step(s):
-            arrive(steps[-1])
+            steps[-1][0].wait_recv()
             a, b = piece(rem(me - (last + 1 - s), n)), piece(rem(me + (last + 1 - s), n))
             if s == 2 and n == 8:
                 add(piece(lax.select(odd, rem(me - 3, n), rem(me + 3, n))), far(0))
             elif s == 2:
                 add(a.at[halves[0]], far(0))
-                add(b.at[halves[1]], far(1))
             else:
                 add(a, full(0, s - 3))
+            first = send(a, full(0, s - 2), left)
+            if s == 2 and n == 4:
+                steps[-1][1].wait_recv()
+                add(b.at[halves[1]], far(1))
+            elif s > 2:
+                steps[-1][1].wait_recv()
                 add(b, full(1, s - 3))
-            steps.append([send(a, full(0, s - 2), left), send(b, full(1, s - 2), right)])
+            steps.append([first, send(b, full(1, s - 2), right)])
 
         def total():
             arrive(steps[-1])

time: 160 us -> 161 us (level)
  no operation moved by 1% of the time
where the time goes in v8:
time: 161 us; the launch traced here: 160 us
  Pallas kernels  159 us (99%)
    pallas_call x1, Pallas kernels, shards(): pl.pallas_call(kernel, out_shape=[jax.ShapeDtypeStruct(*shape) for shape...  156 us

profile of v8, /device:TPU:2, one launch (start us, length us, event | category | flops | bytes accessed | tf_op | source)
XLA Modules:
  0.0 159.8 jit_solution(16438329240137585534)
XLA Ops:
  0.6 156.4 %shard_map.119 = (bf16[2,64,1024]{2,1,0:T(8,128)(2,1)}, bf16[4,4,2,64,128]{4,3,2,1,0:T(8,128)(2,1)}, f32[1024,128]{1,0:T(8,128)}, f32[128,128]{1,0:T(8,128)}, f32[128,1024]{1,0:T(8,128)}) custom-call(bf16[2,64,1024]{2,1,0:T(8,128)(2,1)} %bitcast.14, bf16[4,4,2,64,128]{4,3,2,1,0:T(8,128)(2,1)} %bitcast.11, bf16[2,64,1024]{2,1,0:T(8,128)(2,1)} %bitcast.15, ...), custom_call_target="tpu_custom_call" | custom-call | flops 14000000000 | bytes 5000000 | tf_op jit(solution)/shard_map/pallas_call | solution.py:544
  157.1 2.7 %shard_map.120 = (bf16[128,1024]{1,0:T(8,128)(2,1)}, bf16[2048,128]{1,0:T(8,128)(2,1)}, f32[1024,128]{1,0:T(8,128)}, f32[128,128]{1,0:T(8,128)}, f32[128,1024]{1,0:T(8,128)}) custom-call(bf16[128,1024]{1,0:T(8,128)(2,1)} %bitcast.10, bf16[2048,128]{1,0:T(8,128)(2,1)} %bitcast.9, f32[1024,128]{1,0:T(8,128)} %get-tuple-element.17.refs_2_, ...), custom_call_target="tpu_custom_call" | custom-call | tf_op jit(solution)/shard_map/pallas_call | solution.py:565

commit v9 on v7

--- a/solution.py
+++ b/solution.py
@@ -487,8 +487,20 @@
 
 
 def finish(*refs):
-    for source, target in zip(refs[:5], refs[5:]):
-        target[...] = source[...]
+    sources, targets, held, sems = refs[:5], refs[5:10], refs[10:15], refs[15]
+    loads = [
+        pltpu.make_async_copy(sources[n], held[n], sems.at[n]) for n in range(5)
+    ]
+    stores = [
+        pltpu.make_async_copy(held[n], targets[n], sems.at[5 + n]) for n in range(5)
+    ]
+    for load in loads:
+        load.start()
+    for load, store in zip(loads, stores):
+        load.wait()
+        store.start()
+    for store in stores:
+        store.wait()
 
 
 def shards(layer_input, attn_out, out_grad, q_grad, k_grad, q_weight, k_weight, o_weight):
@@ -557,8 +569,11 @@
     ig, ag, qwg, kwg, owg = pl.pallas_call(
         finish,
         out_shape=[jax.ShapeDtypeStruct(part.shape, part.dtype) for part in parts],
-        in_specs=[pl.BlockSpec(memory_space=pltpu.VMEM)] * 5,
-        out_specs=[pl.BlockSpec(memory_space=pltpu.VMEM)] * 5,
+        in_specs=[pl.BlockSpec(memory_space=pl.ANY)] * 5,
+        out_specs=[pl.BlockSpec(memory_space=pl.ANY)] * 5,
+        scratch_shapes=[pltpu.VMEM(part.shape, part.dtype) for part in parts]
+        + [pltpu.SemaphoreType.DMA((10,))],
+        compiler_params=pltpu.CompilerParams(vmem_limit_bytes=63 * 2**20),
     )(*parts)
     return ig, ag, qwg, kwg[None], owg
 

time: 160 us -> 160 us (level)
  no operation moved by 1% of the time
where the time goes in v9:
time: 160 us
  Pallas kernels  159 us (99%)
    pallas_call x1, Pallas kernels, shards(): pl.pallas_call(kernel, out_shape=[jax.ShapeDtypeStruct(*shape) for shape...  157 us

profile of v9, /device:TPU:2, one launch (start us, length us, event | category | flops | bytes accessed | tf_op | source)
XLA Modules:
  0.0 159.5 jit_solution(7941161962982294225)
XLA Ops:
  0.6 156.5 %shard_map.119 = (bf16[2,64,1024]{2,1,0:T(8,128)(2,1)}, bf16[4,4,2,64,128]{4,3,2,1,0:T(8,128)(2,1)}, f32[1024,128]{1,0:T(8,128)}, f32[128,128]{1,0:T(8,128)}, f32[128,1024]{1,0:T(8,128)}) custom-call(bf16[2,64,1024]{2,1,0:T(8,128)(2,1)} %bitcast.14, bf16[4,4,2,64,128]{4,3,2,1,0:T(8,128)(2,1)} %bitcast.11, bf16[2,64,1024]{2,1,0:T(8,128)(2,1)} %bitcast.15, ...), custom_call_target="tpu_custom_call" | custom-call | flops 14000000000 | bytes 5000000 | tf_op jit(solution)/shard_map/pallas_call | solution.py:548
  157.2 2.4 %shard_map.120 = (bf16[128,1024]{1,0:T(8,128)(2,1)}, bf16[2048,128]{1,0:T(8,128)(2,1)}, f32[1024,128]{1,0:T(8,128)}, f32[128,128]{1,0:T(8,128)}, f32[128,1024]{1,0:T(8,128)}) custom-call(bf16[128,1024]{1,0:T(8,128)(2,1)} %bitcast.10, bf16[2048,128]{1,0:T(8,128)(2,1)} %bitcast.9, f32[1024,128]{1,0:T(8,128)} %get-tuple-element.17.refs_2_, ...), custom_call_target="tpu_custom_call" | custom-call | tf_op jit(solution)/shard_map/pallas_call | solution.py:569
